TPU v7x, 256 devices: a whole 4x4x8 slice. The times are simulated.
256 devices in a mesh: row: 16 (over y, x), col: 16 (over z, core).
Axes of the slice: x: 4, y: 4, z: 8, core: 2. Of those that a mesh axis runs over, the one named last changes fastest.
Arguments:
- activations: bfloat16 [512, 8192], P('col', 'row'), may hold values from -6 to 6
- cotangent: bfloat16 [512, 8192], P('row', 'col'), may hold values from -6 to 6
- gate_base: bfloat16 [8192, 29568], P('row', 'col'), may hold values from -0.0625 to 0.0625
- up_base: bfloat16 [8192, 29568], P('row', 'col'), may hold values from -0.0625 to 0.0625
- down_base: bfloat16 [29568, 8192], P('row', 'col'), may hold values from -0.03125 to 0.03125
- gate_left: float32 [32, 8192], P(None, 'row'), may hold values from -1.75 to 1.75
- gate_right: float32 [32, 29568], P(None, 'col'), may hold values from -1.75 to 1.75
- up_left: float32 [32, 8192], P(None, 'row'), may hold values from -1.75 to 1.75
- up_right: float32 [32, 29568], P(None, 'col'), may hold values from -1.75 to 1.75
- down_left: float32 [32, 29568], P(None, 'row'), may hold values from -1.75 to 1.75
- down_right: float32 [32, 8192], P(None, 'col'), may hold values from -1.75 to 1.75
Outputs:
- grad_input: bfloat16 [512, 8192], P('col', 'row')
- grad_gate_left: float32 [32, 8192], P(None, 'row')
- grad_gate_right: float32 [32, 29568], P(None, 'col')
- grad_up_left: float32 [32, 8192], P(None, 'row')
- grad_up_right: float32 [32, 29568], P(None, 'col')
- grad_down_left: float32 [32, 29568], P(None, 'row')
- grad_down_right: float32 [32, 8192], P(None, 'col')
All inputs are finite; a program needn't handle non-finite values.
Results may differ from a plain program's by a relative error of at most 0.0072.
Values may be sent and summed in bfloat16 or wider, within the bound.
No kernel may reach another device: no remote copies, remote signals or barrier semaphores. Data moves between devices by JAX's collectives and lax.ppermute only.
A program may use at most 128 MiB of HBM per device.

v0:
```python
import jax
import jax.numpy as jnp
from jax import lax
from jax.experimental import pallas as pl
from jax.experimental.pallas import tpu as pltpu
from jax.sharding import Mesh, PartitionSpec as P

F32 = jnp.float32
BF16 = jnp.bfloat16
NY, NX, NZ, NC = 4, 4, 8, 2
ROW = ("y", "x")
COL = ("z", "core")
TILE = 256
LANES = 128
VMEM_LIMIT = 48 * 1024 * 1024
BITREV = (0, 4, 2, 6, 1, 5, 3, 7)


def tiles(width):
    return [(at, min(at + TILE, width)) for at in range(0, width, TILE)]


def kernel_call(body, ids, args, outs, scratch=()):
    return pl.pallas_call(
        body,
        out_shape=[jax.ShapeDtypeStruct(s, d) for s, d in outs],
        in_specs=[pl.BlockSpec(memory_space=pltpu.SMEM)] + [pl.BlockSpec(memory_space=pltpu.VMEM)] * len(args),
        out_specs=[pl.BlockSpec(memory_space=pltpu.VMEM)] * len(outs),
        scratch_shapes=list(scratch),
        compiler_params=pltpu.CompilerParams(vmem_limit_bytes=VMEM_LIMIT),
        cost_estimate=pl.CostEstimate(flops=1024, bytes_accessed=1024, transcendentals=0),
    )(ids, *args)


def plane_permute(v, move, primary):
    perm = []
    for y in range(NY):
        for x in range(NX):
            for core in range(NC):
                on_x = (core == 0) == primary
                ty, tx = (y, move(x)) if on_x else (move(y), x)
                perm.append(((y * NX + x) * NC + core, (ty * NX + tx) * NC + core))
    return lax.ppermute(v, ("y", "x", "core"), perm)


def plane_shift(v, step, primary):
    return plane_permute(v, lambda i: (i + step) % 4, primary)


def z_swap(v, mask):
    return lax.ppermute(v, "z", [(i, i ^ mask) for i in range(NZ)])


def core_swap(v):
    return lax.ppermute(v, "core", [(0, 1), (1, 0)])


def to_columns(v):
    perm = [(j * 16 + b, (b ^ j) * 16 + j) for j in range(16) for b in range(16)]
    return lax.ppermute(v, ("y", "x", "z", "core"), perm)


def to_rows(v):
    perm = [(a * 16 + j, j * 16 + (a ^ j)) for a in range(16) for j in range(16)]
    return lax.ppermute(v, ("y", "x", "z", "core"), perm)


def to_all(v, axis):
    return lax.all_to_all(v, axis, split_axis=0, concat_axis=0, tiled=True)


def add_all(*vs):
    total = vs[0].astype(F32)
    for v in vs[1:]:
        total = total + v.astype(F32)
    return total


def swish_parts(gate_z, up_z, grad_h):
    squash = jax.nn.sigmoid(gate_z)
    swished = gate_z * squash
    hidden = (swished * up_z).astype(BF16)
    d_up = (grad_h * swished).astype(BF16)
    d_gate = (grad_h * up_z * squash * (1.0 + gate_z * (1.0 - squash))).astype(BF16)
    return hidden, d_gate, d_up


def nt(a, b):
    return lax.dot_general(a, b, (((1,), (1,)), ((), ())), preferred_element_type=F32)


def tn(a, b):
    return lax.dot_general(a, b, (((0,), (0,)), ((), ())), preferred_element_type=F32)


def nn(a, b):
    return jnp.dot(a, b, preferred_element_type=F32)


def split(v):
    high = v.astype(BF16)
    return high, (v - high.astype(F32)).astype(BF16)


def hilo(v):
    return jnp.concatenate(split(v), axis=0)


def plane_block(ids, at):
    y, x, z, core = ids[0], ids[1], ids[2], ids[3]
    one, two = at // 4, at % 4
    dx = jnp.where(core == 0, one, two)
    dy = jnp.where(core == 0, two, one)
    return (((y + dy) & 3) * 4 + ((x + dx) & 3)) ^ (z * 2 + core)


def slot_of(off):
    return ((off & 1) << 2) | (off & 2) | (off >> 2)


def eff_body(ids, *refs):
    n = len(refs) // 4
    for base, wide, narrow, eff in zip(refs[:n], refs[n : 2 * n], refs[2 * n : 3 * n], refs[3 * n :]):
        nh, nl = split(narrow[...])
        n3 = jnp.concatenate([nh, nh, nl], axis=0)
        for lo, hi in tiles(base.shape[0]):
            wh, wl = split(wide[:, lo:hi])
            lowrank = tn(jnp.concatenate([wh, wl, wh], axis=0), n3)
            eff[lo:hi, :] = (base[lo:hi, :].astype(F32) * (1.0 + lowrank)).astype(BF16)


def hid_body(ids, cot, eff, own, other, rel):
    core = ids[3]
    for k in range(2):
        for n in range(8):
            at = (k * 8 + n) * 32
            rel[at : at + 32, :] = cot[n * 2 + (core ^ k)]
    a = rel[...]
    for lo, hi in tiles(eff.shape[0]):
        r = nt(a, eff[lo:hi, :])
        own[:, :, lo:hi] = r[:256].reshape(8, 32, hi - lo).astype(BF16)
        other[:, :, lo:hi] = r[256:].reshape(8, 32, hi - lo).astype(BF16)


def sum_body(ids, act_own, act_other, gate_eff, up_eff, c0, c1, c2, c3, rel, act):
    z, core = ids[2], ids[3]
    act[core] = act_own[...]
    act[1 - core] = act_other[...]
    for at in range(16):
        block = plane_block(ids, at)
        rel[at * 32 : at * 32 + 32, :] = act[block & 1, slot_of((block >> 1) ^ z)]
    a = rel[...]
    for m, eff in enumerate((gate_eff, up_eff)):
        for lo, hi in tiles(eff.shape[0]):
            r = nt(a, eff[lo:hi, :])
            for k, out in enumerate((c0, c1, c2, c3)):
                part = r[k * 128 : (k + 1) * 128].reshape(4, 32, hi - lo)
                out[:, m, :, lo:hi] = part.astype(out.dtype)


def store_tiles(out, start, blocks, lane, v):
    width = v.shape[1]
    pad = -width % LANES
    if pad:
        v = jnp.concatenate([v, jnp.zeros((32, pad), F32)], axis=1)
    for j in range(v.shape[1] // LANES):
        for g in range(4):
            out[start + g * blocks + lane // LANES + j] = v[g * 8 : g * 8 + 8, j * LANES : (j + 1) * LANES]


def load_tiles(v, start, width):
    blocks = -(-width // LANES)
    v = v[start : start + 4 * blocks].reshape(4, blocks, 8, LANES)
    return v.swapaxes(1, 2).reshape(32, blocks * LANES)[:, :width]


def grad_body(ids, g0, g1, g2, g3, rel, *refs):
    bases, effs, wides, narrows = refs[0:2], refs[2:4], refs[4:6], refs[6:8]
    gi, left, right, acc = refs[8:]
    a = rel[...]
    dm = rel.shape[1]
    for m in range(2):
        base, eff, wide, narrow = bases[m], effs[m], wides[m], narrows[m]
        width = base.shape[0]
        blocks = -(-width // LANES)
        n2 = hilo(narrow[...])
        total = jnp.zeros((64, dm), F32)
        for n, (lo, hi) in enumerate(tiles(width)):
            g = jnp.concatenate([r[:, m, :, lo:hi].reshape(128, hi - lo) for r in (g0, g1, g2, g3)], axis=0)
            term = nn(g, eff[lo:hi, :])
            masked = (tn(g, a) * base[lo:hi, :].astype(F32)).astype(BF16)
            rp = nt(n2, masked)
            total = total + nn(hilo(wide[:, lo:hi]), masked)
            store_tiles(right, m * 4 * blocks, blocks, lo, rp[:32] + rp[32:])
            if n == 0 and m == 0:
                acc[...] = term
            else:
                acc[...] += term
        store_tiles(left, m * dm // 32, dm // LANES, 0, total[:32] + total[32:])
    z, core = ids[2], ids[3]
    for at in range(16):
        block = plane_block(ids, at)
        slot = slot_of((block >> 1) ^ z)
        for g in range(4):
            row = at * 32 + g * 8
            for j in range(dm // LANES):
                piece = acc[row : row + 8, j * LANES : (j + 1) * LANES]
                gi[(block & 1) ^ core, slot, g * (dm // LANES) + j] = piece


def down_grad_body(ids, hid_own, hid_other, cot, base, wide, narrow, left, right, rel):
    core = ids[3]
    for k in range(2):
        for n in range(8):
            at = (k * 8 + n) * 32
            rel[at : at + 32, :] = cot[n * 2 + (core ^ k)]
    c = rel[...]
    n2 = hilo(narrow[...])
    width, dm = base.shape
    blocks = -(-width // LANES)
    total = jnp.zeros((64, dm), F32)
    for lo, hi in tiles(width):
        h = jnp.concatenate([r[:, :, lo:hi].reshape(256, hi - lo) for r in (hid_own, hid_other)], axis=0)
        masked = (tn(h, c) * base[lo:hi, :].astype(F32)).astype(BF16)
        lp = nt(n2, masked)
        total = total + nn(hilo(wide[:, lo:hi]), masked)
        store_tiles(left, 0, blocks, lo, lp[:32] + lp[32:])
    store_tiles(right, 0, dm // LANES, 0, total[:32] + total[32:])


def scatter4(chunks, primary):
    return [chunks[0]] + [plane_shift(chunks[k], k, primary) for k in (1, 2, 3)]


def gather4(v, primary):
    return [v] + [plane_shift(v, -k, primary) for k in (1, 2, 3)]


def per_device(
    activations,
    cotangent,
    gate_base,
    up_base,
    down_base,
    gate_left,
    gate_right,
    up_left,
    up_right,
    down_left,
    down_right,
):
    ids = jnp.stack([lax.axis_index(a) for a in ("y", "x", "z", "core")]).astype(jnp.int32)
    dm, ff = gate_base.shape
    gate_t, up_t = gate_base.T, up_base.T

    cot = to_all(jnp.broadcast_to(cotangent[None], (16,) + cotangent.shape), ROW)
    act_own = activations[None]
    for mask in (4, 2, 1):
        act_own = jnp.concatenate([act_own, z_swap(act_own, mask)], axis=0)
    (down_eff,) = kernel_call(eff_body, ids, [down_base, down_left, down_right], [((ff, dm), BF16)])
    ids, act_own = lax.optimization_barrier((ids, act_own))
    act_other = core_swap(act_own)
    gate_eff, up_eff = kernel_call(
        eff_body, ids, [gate_t, up_t, gate_right, up_right, gate_left, up_left], [((ff, dm), BF16)] * 2
    )
    h_own, h_other = kernel_call(
        hid_body,
        ids,
        [cot, down_eff],
        [((8, 32, ff), BF16)] * 2,
        scratch=[pltpu.VMEM((512, dm), BF16)],
    )
    h_pair = add_all(h_own, core_swap(h_other)).astype(BF16)
    act_own, act_other, h_pair = lax.optimization_barrier((act_own, act_other, h_pair))
    *chunks, act_rel = kernel_call(
        sum_body,
        ids,
        [act_own, act_other, gate_eff, up_eff],
        [((4, 2, 32, ff), BF16)] * 4 + [((512, dm), BF16)],
        scratch=[pltpu.VMEM((2, 8, 32, dm), BF16)],
    )
    grad_h = jnp.sum(to_all(h_pair, "z").astype(F32), axis=0)
    grad_h = to_columns(grad_h.astype(BF16)).astype(F32)

    got = scatter4(chunks, True)
    parts = [add_all(*[g[k] for g in got]) for k in range(4)]
    zs = add_all(*scatter4([parts[0]] + [p.astype(BF16) for p in parts[1:]], False))

    hidden, d_gate, d_up = swish_parts(zs[0], zs[1], grad_h)
    hid = to_rows(hidden)
    near = jnp.stack(gather4(jnp.stack([d_gate, d_up]), False))
    near, hid = lax.optimization_barrier((near, hid))
    grads = gather4(near, True)
    hid_own = to_all(jnp.broadcast_to(hid[None], (NZ,) + hid.shape), "z")
    hid_other = core_swap(hid_own)

    wide_tiles, narrow_tiles = 4 * -(-ff // LANES), dm // 32
    gi, l_up, r_up = kernel_call(
        grad_body,
        ids,
        [*grads, act_rel, gate_t, up_t, gate_eff, up_eff, gate_right, up_right, gate_left, up_left],
        [
            ((2, 8, narrow_tiles, 8, LANES), F32),
            ((2 * narrow_tiles, 8, LANES), F32),
            ((2 * wide_tiles, 8, LANES), F32),
        ],
        scratch=[pltpu.VMEM((512, dm), F32)],
    )
    l_down, r_down = kernel_call(
        down_grad_body,
        ids,
        [hid_own, hid_other, cot, down_base, down_left, down_right],
        [((wide_tiles, 8, LANES), F32), ((narrow_tiles, 8, LANES), F32)],
        scratch=[pltpu.VMEM((512, dm), BF16)],
    )

    r_all = jnp.concatenate([r_up, r_down], axis=0)
    for primary in (True, False):
        r_all = r_all + add_all(*gather4(r_all.astype(BF16), primary)[1:])

    first = lax.axis_index("core") == 0
    l_all = jnp.concatenate([l_up, l_down], axis=0)
    half = l_all.shape[0] // 2
    low, high = l_all[:half], l_all[half:]
    mine, theirs = jnp.where(first, low, high), jnp.where(first, high, low)
    n = 8 * gi.shape[2]
    both = core_swap(jnp.concatenate([gi[1].reshape(n, 8, LANES), theirs], axis=0))
    gi, l_sum = gi[0].reshape(n, 8, LANES) + both[:n], mine + both[n:]
    for mask in (1, 2, 4):
        n = n // 2
        both = z_swap(jnp.concatenate([gi[n:], l_sum], axis=0).astype(BF16), mask).astype(F32)
        gi, l_sum = gi[:n] + both[:n], l_sum + both[n:]
    grad_input = load_tiles(gi, 0, dm).astype(BF16)
    l_other = core_swap(l_sum)
    l_all = jnp.concatenate([jnp.where(first, l_sum, l_other), jnp.where(first, l_other, l_sum)], axis=0)
    gate_l = load_tiles(l_all, 0, dm)
    up_l = load_tiles(l_all, narrow_tiles, dm)
    down_l = load_tiles(l_all, 2 * narrow_tiles, ff)
    gate_r = load_tiles(r_all, 0, ff)
    up_r = load_tiles(r_all, wide_tiles, ff)
    down_r = load_tiles(r_all, 2 * wide_tiles, dm)
    return (grad_input, gate_l, gate_r, up_l, up_r, down_l, down_r)


def solution(mesh):
    fine = Mesh(mesh.devices.reshape(NY, NX, NZ, NC), ("y", "x", "z", "core"))
    both, left, right = P(ROW, COL), P(None, ROW), P(None, COL)
    return jax.shard_map(
        per_device,
        mesh=fine,
        in_specs=(P(COL, ROW), both, both, both, both, left, right, left, right, left, right),
        out_specs=(P(COL, ROW), left, right, left, right, left, right),
        check_vma=False,
    )
```

profile of v0, /device:TPU:1, one launch (start us, length us, event | category | flops | bytes accessed | tf_op | source)
XLA Modules:
  0.0 220.8 jit_solution(13484769277779803622)
XLA Ops:
  0.7 7.8 %collective-permute-start = (bf16[1,32,512]{2,1,0:T(8,128)(2,1)}, bf16[1,32,512]{2,1,0:T(8,128)(2,1)S(1)}, u32[]{:S(2)}, u32[]{:S(2)}) collective-permute-start(bf16[1,32,512]{2,1,0:T(8,128)(2,1)} %bitcast.94), channel_id=1, source_target_pairs={{0,8},{2,10},{4,12},{6,14},{8,0},{10,2},{12,4},{14,6},{1,9},{3,11}... | collective-permute-start | bytes 98312 | tf_op jit(solution)/shard_map/ppermute | solution.py:51
  8.5 1.6 broadcast_in_dim.7
  10.1 6.8 %all-to-all-start = ((bf16[16,32,512]{2,1,0:T(8,128)(2,1)}), bf16[16,32,512]{2,1,0:T(8,128)(2,1)S(1)}, u32[]{:S(2)}, u32[]{:S(2)}) async-start(bf16[16,32,512]{2,1,0:T(8,128)(2,1)} %broadcast_in_dim.7), calls=%async_computation | async-start | bytes 1048576 | tf_op jit(solution)/shard_map/all_to_all | solution.py:69
  17.6 1.2 collective-permute-start.1
  18.8 3.8 %collective-permute-done.1 = bf16[2,32,512]{2,1,0:T(8,128)(2,1)S(1)} collective-permute-done((bf16[2,32,512]{2,1,0:T(8,128)(2,1)S(1)}, bf16[2,32,512]{2,1,0:T(8,128)(2,1)S(1)}, u32[]{:S(2)}, u32[]{:S(2)}) %collective-permute-start.1) | collective-permute-done | bytes 65568 | tf_op jit(solution)/shard_map/ppermute | solution.py:51
  24.6 1.2 shard_map.162.eff
  25.8 1.3 copy-done.3
  27.7 1.5 copy-done.4
  29.2 1.8 shard_map.163
  31.0 3.0 %collective-permute-start.4 = (bf16[8,32,1848]{2,1,0:T(8,128)(2,1)S(1)}, bf16[8,32,1848]{2,1,0:T(8,128)(2,1)S(1)}, u32[]{:S(2)}, u32[]{:S(2)}) collective-permute-start(bf16[8,32,1848]{2,1,0:T(8,128)(2,1)S(1)} %get-tuple-element.31), channel_id=1, source_target_pairs={{0,1},{1,0},{2,3},{3,2},{4,5},{5,4},{6,7},{7,6},{8,9},{9,8},{10,11... | collective-permute-start | bytes 2838536 | tf_op jit(solution)/shard_map/ppermute | solution.py:55
  34.2 3.3 %shard_map.164 = (bf16[1848,512]{1,0:T(8,128)(2,1)S(1)}, bf16[1848,512]{1,0:T(8,128)(2,1)S(1)}) custom-call(s32[4]{0:T(128)S(1)} %pad_add_fusion.ids, bf16[1848,512]{1,0:T(8,128)(2,1)} %bitcast.89, bf16[1848,512]{1,0:T(8,128)(2,1)} %bitcast.91, f32[32,1848]{1,0:T(8,128)S(1)} %copy-done.8, f32[32,1848]{1,0:T(8,128)S(1)} %copy-done.10, ...), custom_call_target="tpu_custom_call" | custom-call | flops 1024 | bytes 1024 | tf_op jit(solution)/shard_map/pallas_call | solution.py:24
  37.4 1.3 copy-done
  38.7 1.3 copy-done.1
  40.0 1.2 add_convert_fusion
  41.2 6.0 %shard_map.165 = (bf16[4,2,32,1848]{3,2,1,0:T(8,128)(2,1)S(1)}, bf16[4,2,32,1848]{3,2,1,0:T(8,128)(2,1)}, bf16[4,2,32,1848]{3,2,1,0:T(8,128)(2,1)}, bf16[4,2,32,1848]{3,2,1,0:T(8,128)(2,1)}, bf16[512,512]{1,0:T(8,128)(2,1)S(1)}) custom-call(s32[4]{0:T(128)S(1)} %pad_add_fusion.ids, bf16[8,32,512]{2,1,0:T(8,128)(2,1)S(1)} %pad_maximum_fusion.2.act_own, ...), custom_call_target="tpu_custom_call" | custom-call | flops 1024 | bytes 1024 | tf_op jit(solution)/shard_map/pallas_call | solution.py:24
  49.0 1.6 collective-permute-start.6
  50.7 2.4 %collective-permute-start.7 = (bf16[4,2,32,1848]{3,2,1,0:T(8,128)(2,1)}, bf16[4,2,32,1848]{3,2,1,0:T(8,128)(2,1)}, u32[]{:S(2)}, u32[]{:S(2)}) collective-permute-start(bf16[4,2,32,1848]{3,2,1,0:T(8,128)(2,1)} %get-tuple-element.39), channel_id=1, source_target_pairs={{0,32},{1,129},{16,48},{17,145},{32,0},{33,161},{48,16},{49,177},{... | collective-permute-start | bytes 2838536 | tf_op jit(solution)/shard_map/ppermute | solution.py:43
  54.3 4.3 %all-to-all-start.1 = ((bf16[8,32,1848]{2,1,0:T(8,128)(2,1)}), bf16[8,32,1848]{2,1,0:T(8,128)(2,1)}, u32[]{:S(2)}, u32[]{:S(2)}) async-start(bf16[8,32,1848]{2,1,0:T(8,128)(2,1)} %add_convert_fusion), calls=%async_computation.1 | async-start | bytes 1966080 | tf_op jit(solution)/shard_map/all_to_all | solution.py:69
  58.5 5.5 %collective-permute-done.6 = bf16[4,2,32,1848]{3,2,1,0:T(8,128)(2,1)} collective-permute-done((bf16[4,2,32,1848]{3,2,1,0:T(8,128)(2,1)}, bf16[4,2,32,1848]{3,2,1,0:T(8,128)(2,1)}, u32[]{:S(2)}, u32[]{:S(2)}) %collective-permute-start.6) | collective-permute-done | bytes 946208 | tf_op jit(solution)/shard_map/ppermute | solution.py:43
  64.0 11.7 %collective-permute-done.7 = bf16[4,2,32,1848]{3,2,1,0:T(8,128)(2,1)} collective-permute-done((bf16[4,2,32,1848]{3,2,1,0:T(8,128)(2,1)}, bf16[4,2,32,1848]{3,2,1,0:T(8,128)(2,1)}, u32[]{:S(2)}, u32[]{:S(2)}) %collective-permute-start.7) | collective-permute-done | bytes 946208 | tf_op jit(solution)/shard_map/ppermute | solution.py:43
  75.7 2.8 %fusion.6 = (bf16[2,32,1848]{2,1,0:T(8,128)(2,1)}, bf16[2,32,1848]{2,1,0:T(8,128)(2,1)}, bf16[2,32,1848]{2,1,0:T(8,128)(2,1)}) fusion(bf16[4,2,32,1848]{3,2,1,0:T(8,128)(2,1)} %collective-permute-done.8, bf16[4,2,32,1848]{3,2,1,0:T(8,128)(2,1)} %collective-permute-done.7, bf16[4,2,32,1848]{3,2,1,0:T(8,128)(2,1)} %collective-permute-done.6, ...), kind=kLoop, calls=%fused_computation.21 | loop fusion | flops 2838528 | bytes 3548160 | tf_op jit(solution)/shard_map/add | solution.py:75
  79.7 1.5 collective-permute-start.11
  82.4 1.7 all-to-all-done.1
  84.1 2.0 reduce_sum.12
  86.2 5.6 %collective-permute-start.5 = (bf16[32,1848]{1,0:T(8,128)(2,1)}, bf16[32,1848]{1,0:T(8,128)(2,1)S(1)}, u32[]{:S(2)}, u32[]{:S(2)}) collective-permute-start(bf16[32,1848]{1,0:T(8,128)(2,1)} %reduce_sum.12), channel_id=1, source_target_pairs={{0,0},{1,16},{2,32},{3,48},{4,64},{5,80},{6,96},{7,112},{8,128},{9... | collective-permute-start | bytes 354824 | tf_op jit(solution)/shard_map/ppermute | solution.py:60
  91.8 1.7 fusion.1
  94.2 10.5 %collective-permute-start.13 = (bf16[2,32,1848]{2,1,0:T(8,128)(2,1)S(1)}, bf16[2,32,1848]{2,1,0:T(8,128)(2,1)S(1)}, u32[]{:S(2)}, u32[]{:S(2)}) collective-permute-start(bf16[2,32,1848]{2,1,0:T(8,128)(2,1)S(1)} %get-tuple-element.64), channel_id=1, source_target_pairs={{0,128},{1,33},{16,144},{17,49},{32,160},{33,1},{48,176},{49,17},{... | collective-permute-start | bytes 709640 | tf_op jit(solution)/shard_map/ppermute | solution.py:43
  104.6 2.4 %collective-permute-start.12 = (bf16[2,32,1848]{2,1,0:T(8,128)(2,1)S(1)}, bf16[2,32,1848]{2,1,0:T(8,128)(2,1)S(1)}, u32[]{:S(2)}, u32[]{:S(2)}) collective-permute-start(bf16[2,32,1848]{2,1,0:T(8,128)(2,1)S(1)} %get-tuple-element.64), channel_id=1, source_target_pairs={{0,192},{1,49},{16,208},{17,1},{32,224},{33,17},{48,240},{49,33},{... | collective-permute-start | bytes 709640 | tf_op jit(solution)/shard_map/ppermute | solution.py:43
  107.5 3.4 %collective-permute-start.15 = (bf16[32,1848]{1,0:T(8,128)(2,1)S(1)}, bf16[32,1848]{1,0:T(8,128)(2,1)S(1)}, u32[]{:S(2)}, u32[]{:S(2)}) collective-permute-start(bf16[32,1848]{1,0:T(8,128)(2,1)S(1)} %get-tuple-element.60), channel_id=1, source_target_pairs={{0,0},{1,17},{2,34},{3,51},{4,68},{5,85},{6,102},{7,119},{8,136},{... | collective-permute-start | bytes 354824 | tf_op jit(solution)/shard_map/ppermute | solution.py:65
  110.9 3.2 %collective-permute-done.12 = bf16[2,32,1848]{2,1,0:T(8,128)(2,1)S(1)} collective-permute-done((bf16[2,32,1848]{2,1,0:T(8,128)(2,1)S(1)}, bf16[2,32,1848]{2,1,0:T(8,128)(2,1)S(1)}, u32[]{:S(2)}, u32[]{:S(2)}) %collective-permute-start.12) | collective-permute-done | bytes 236576 | tf_op jit(solution)/shard_map/ppermute | solution.py:43
  116.6 11.4 %all-to-all-start.2 = ((bf16[8,32,1848]{2,1,0:T(8,128)(2,1)}), bf16[8,32,1848]{2,1,0:T(8,128)(2,1)S(1)}, u32[]{:S(2)}, u32[]{:S(2)}) async-start(bf16[8,32,1848]{2,1,0:T(8,128)(2,1)} %broadcast_in_dim.8), calls=%async_computation.2 | async-start | bytes 1966080 | tf_op jit(solution)/shard_map/all_to_all | solution.py:69
  128.9 1.9 collective-permute-start.16
  130.7 25.1 %all-to-all-done.2.hid_own = bf16[8,32,1848]{2,1,0:T(8,128)(2,1)S(1)} async-done(((bf16[8,32,1848]{2,1,0:T(8,128)(2,1)}), bf16[8,32,1848]{2,1,0:T(8,128)(2,1)S(1)}, u32[]{:S(2)}, u32[]{:S(2)}) %all-to-all-start.2) | async-done | bytes 946208 | tf_op jit(solution)/shard_map/all_to_all | solution.py:69
  156.3 1.2 copy-done.5
  160.5 12.8 %shard_map.166 = (f32[2,8,16,8,128]{4,3,2,1,0:T(8,128)}, f32[32,8,128]{2,1,0:T(8,128)S(1)}, f32[120,8,128]{2,1,0:T(8,128)S(1)}) custom-call(s32[4]{0:T(128)S(1)} %pad_add_fusion.ids, bf16[4,2,32,1848]{3,2,1,0:T(8,128)(2,1)S(1)} %copy-done.5, bf16[4,2,32,1848]{3,2,1,0:T(8,128)(2,1)} %collective-permute-done.16.g1, ...), custom_call_target="tpu_custom_call" | custom-call | flops 1024 | bytes 1024 | tf_op jit(solution)/shard_map/pallas_call | solution.py:24
  173.3 1.3 fusion.18
  174.7 4.2 %shard_map.167 = (f32[60,8,128]{2,1,0:T(8,128)S(1)}, f32[16,8,128]{2,1,0:T(8,128)S(1)}) custom-call(s32[4]{0:T(128)S(1)} %pad_add_fusion.ids, bf16[8,32,1848]{2,1,0:T(8,128)(2,1)S(1)} %all-to-all-done.2.hid_own, bf16[8,32,1848]{2,1,0:T(8,128)(2,1)} %collective-permute-done.19.hid_other, bf16[16,32,512]{2,1,0:T(8,128)(2,1)S(1)} %all-to-all-done.cot, ...), custom_call_target="tpu_custom_call" | custom-call | flops 1024 | bytes 1024 | tf_op jit(solution)/shard_map/pallas_call | solution.py:24
  179.4 2.2 collective-permute-start.26
  182.1 1.7 collective-permute-start.21
  183.8 5.4 %collective-permute-done.27 = bf16[136,8,128]{2,1,0:T(8,128)(2,1)S(1)} collective-permute-done((bf16[136,8,128]{2,1,0:T(8,128)(2,1)S(1)}, bf16[136,8,128]{2,1,0:T(8,128)(2,1)S(1)}, u32[]{:S(2)}, u32[]{:S(2)}) %collective-permute-start.27) | collective-permute-done | bytes 278560 | tf_op jit(solution)/shard_map/ppermute | solution.py:43
  189.9 1.6 collective-permute-start.30
  191.5 2.3 %collective-permute-start.29 = (bf16[136,8,128]{2,1,0:T(8,128)(2,1)S(1)}, bf16[136,8,128]{2,1,0:T(8,128)(2,1)S(1)}, u32[]{:S(2)}, u32[]{:S(2)}) collective-permute-start(bf16[136,8,128]{2,1,0:T(8,128)(2,1)S(1)} %fusion.14), channel_id=1, source_target_pairs={{0,128},{1,33},{16,144},{17,49},{32,160},{33,1},{48,176},{49,17},{... | collective-permute-start | bytes 835592 | tf_op jit(solution)/shard_map/ppermute | solution.py:43
  194.8 2.7 %collective-permute-start.22 = (bf16[78,8,128]{2,1,0:T(8,128)(2,1)S(1)}, bf16[78,8,128]{2,1,0:T(8,128)(2,1)S(1)}, u32[]{:S(2)}, u32[]{:S(2)}) collective-permute-start(bf16[78,8,128]{2,1,0:T(8,128)(2,1)S(1)} %pad_maximum_fusion.7), channel_id=1, source_target_pairs={{0,4},{2,6},{4,0},{6,2},{8,12},{10,14},{12,8},{14,10},{1,5},{3,7},... | collective-permute-start | bytes 479240 | tf_op jit(solution)/shard_map/ppermute | solution.py:51
  197.5 3.5 %collective-permute-done.29 = bf16[136,8,128]{2,1,0:T(8,128)(2,1)S(1)} collective-permute-done((bf16[136,8,128]{2,1,0:T(8,128)(2,1)S(1)}, bf16[136,8,128]{2,1,0:T(8,128)(2,1)S(1)}, u32[]{:S(2)}, u32[]{:S(2)}) %collective-permute-start.29) | collective-permute-done | bytes 278560 | tf_op jit(solution)/shard_map/ppermute | solution.py:43
  201.9 3.1 %collective-permute-done.22 = bf16[78,8,128]{2,1,0:T(8,128)(2,1)S(1)} collective-permute-done((bf16[78,8,128]{2,1,0:T(8,128)(2,1)S(1)}, bf16[78,8,128]{2,1,0:T(8,128)(2,1)S(1)}, u32[]{:S(2)}, u32[]{:S(2)}) %collective-permute-start.22) | collective-permute-done | bytes 159776 | tf_op jit(solution)/shard_map/ppermute | solution.py:51
  205.1 6.0 %collective-permute-start.23 = (bf16[62,8,128]{2,1,0:T(8,128)(2,1)S(1)}, bf16[62,8,128]{2,1,0:T(8,128)(2,1)S(1)}, u32[]{:S(2)}, u32[]{:S(2)}) collective-permute-start(bf16[62,8,128]{2,1,0:T(8,128)(2,1)S(1)} %pad_maximum_fusion.9), channel_id=1, source_target_pairs={{0,8},{2,10},{4,12},{6,14},{8,0},{10,2},{12,4},{14,6},{1,9},{3,11}... | collective-permute-start | bytes 380936 | tf_op jit(solution)/shard_map/ppermute | solution.py:51
  211.9 2.2 %collective-permute-done.23 = bf16[62,8,128]{2,1,0:T(8,128)(2,1)S(1)} collective-permute-done((bf16[62,8,128]{2,1,0:T(8,128)(2,1)S(1)}, bf16[62,8,128]{2,1,0:T(8,128)(2,1)S(1)}, u32[]{:S(2)}, u32[]{:S(2)}) %collective-permute-start.23) | collective-permute-done | bytes 127008 | tf_op jit(solution)/shard_map/ppermute | solution.py:51
  214.2 4.2 %collective-permute-start.24 = (f32[46,8,128]{2,1,0:T(8,128)S(1)}, f32[46,8,128]{2,1,0:T(8,128)S(1)}, u32[]{:S(2)}, u32[]{:S(2)}) collective-permute-start(f32[46,8,128]{2,1,0:T(8,128)S(1)} %slice_add_fusion.2), channel_id=1, source_target_pairs={{0,1},{1,0},{2,3},{3,2},{4,5},{5,4},{6,7},{7,6},{8,9},{9,8},{10,11... | collective-permute-start | bytes 565256 | tf_op jit(solution)/shard_map/ppermute | solution.py:55
  (111 shorter events, 23.6 us)
Async XLA Ops:
  0.6 23.0 %copy-start.18 = (f32[32,512]{1,0:T(8,128)S(1)}, f32[32,512]{1,0:T(8,128)}, u32[]{:S(2)}) copy-start(f32[32,512]{1,0:T(8,128)} %narrow.1) | copy-start | bytes 196612
  0.6 23.0 %copy-start.2 = (bf16[1848,512]{1,0:T(8,128)(2,1)S(1)}, bf16[1848,512]{1,0:T(8,128)(2,1)}, u32[]{:S(2)}) copy-start(bf16[1848,512]{1,0:T(8,128)(2,1)} %base.1) | copy-start | bytes 5677060
  0.7 16.2 %collective-permute-start = (bf16[1,32,512]{2,1,0:T(8,128)(2,1)}, bf16[1,32,512]{2,1,0:T(8,128)(2,1)S(1)}, u32[]{:S(2)}, u32[]{:S(2)}) collective-permute-start(bf16[1,32,512]{2,1,0:T(8,128)(2,1)} %bitcast.94), channel_id=1, source_target_pairs={{0,8},{2,10},{4,12},{6,14},{8,0},{10,2},{12,4},{14,6},{1,9},{3,11}... | collective-permute-start | bytes 98312 | tf_op jit(solution)/shard_map/ppermute | solution.py:51
  10.1 17.6 %all-to-all-start = ((bf16[16,32,512]{2,1,0:T(8,128)(2,1)}), bf16[16,32,512]{2,1,0:T(8,128)(2,1)S(1)}, u32[]{:S(2)}, u32[]{:S(2)}) async-start(bf16[16,32,512]{2,1,0:T(8,128)(2,1)} %broadcast_in_dim.7), calls=%async_computation | async-start | bytes 1048576 | tf_op jit(solution)/shard_map/all_to_all | solution.py:69
  17.6 5.0 %collective-permute-start.1 = (bf16[2,32,512]{2,1,0:T(8,128)(2,1)S(1)}, bf16[2,32,512]{2,1,0:T(8,128)(2,1)S(1)}, u32[]{:S(2)}, u32[]{:S(2)}) collective-permute-start(bf16[2,32,512]{2,1,0:T(8,128)(2,1)S(1)} %pad_maximum_fusion.10), channel_id=1, source_target_pairs={{0,4},{2,6},{4,0},{6,2},{8,12},{10,14},{12,8},{14,10},{1,5},{3,7},... | collective-permute-start | bytes 196616 | tf_op jit(solution)/shard_map/ppermute | solution.py:51
  23.4 4.2 %collective-permute-start.2 = (bf16[4,32,512]{2,1,0:T(8,128)(2,1)S(1)}, bf16[4,32,512]{2,1,0:T(8,128)(2,1)S(1)}, u32[]{:S(2)}, u32[]{:S(2)}) collective-permute-start(bf16[4,32,512]{2,1,0:T(8,128)(2,1)S(1)} %pad_maximum_fusion.8), channel_id=1, source_target_pairs={{0,2},{2,0},{4,6},{6,4},{8,10},{10,8},{12,14},{14,12},{1,3},{3,1},... | collective-permute-start | bytes 393224 | tf_op jit(solution)/shard_map/ppermute | solution.py:51
  24.6 3.1 %copy-start.20 = (bf16[32,512]{1,0:T(8,128)(2,1)S(1)}, bf16[32,512]{1,0:T(8,128)(2,1)}, u32[]{:S(2)}) copy-start(bf16[32,512]{1,0:T(8,128)(2,1)} %param.11) | copy-start | bytes 98308
  24.6 9.6 %copy-start.16 = (f32[32,512]{1,0:T(8,128)S(1)}, f32[32,512]{1,0:T(8,128)}, u32[]{:S(2)}) copy-start(f32[32,512]{1,0:T(8,128)} %refs_6_.1) | copy-start | bytes 196612
  24.6 9.6 %copy-start.17 = (f32[32,512]{1,0:T(8,128)S(1)}, f32[32,512]{1,0:T(8,128)}, u32[]{:S(2)}) copy-start(f32[32,512]{1,0:T(8,128)} %refs_7_.1) | copy-start | bytes 196612
  25.8 1.3 copy-start.3
  27.1 7.1 %copy-start.8 = (f32[32,1848]{1,0:T(8,128)S(1)}, f32[32,1848]{1,0:T(8,128)}, u32[]{:S(2)}) copy-start(f32[32,1848]{1,0:T(8,128)} %refs_4_.3) | copy-start | bytes 709636
  27.1 7.1 %copy-start.10 = (f32[32,1848]{1,0:T(8,128)S(1)}, f32[32,1848]{1,0:T(8,128)}, u32[]{:S(2)}) copy-start(f32[32,1848]{1,0:T(8,128)} %refs_5_.3) | copy-start | bytes 709636
  27.7 1.5 copy-start.4
  31.0 9.0 %collective-permute-start.4 = (bf16[8,32,1848]{2,1,0:T(8,128)(2,1)S(1)}, bf16[8,32,1848]{2,1,0:T(8,128)(2,1)S(1)}, u32[]{:S(2)}, u32[]{:S(2)}) collective-permute-start(bf16[8,32,1848]{2,1,0:T(8,128)(2,1)S(1)} %get-tuple-element.31), channel_id=1, source_target_pairs={{0,1},{1,0},{2,3},{3,2},{4,5},{5,4},{6,7},{7,6},{8,9},{9,8},{10,11... | collective-permute-start | bytes 2838536 | tf_op jit(solution)/shard_map/ppermute | solution.py:55
  34.0 7.2 %collective-permute-start.3 = (bf16[8,32,512]{2,1,0:T(8,128)(2,1)S(1)}, bf16[8,32,512]{2,1,0:T(8,128)(2,1)S(1)}, u32[]{:S(2)}, u32[]{:S(2)}) collective-permute-start(bf16[8,32,512]{2,1,0:T(8,128)(2,1)S(1)} %pad_maximum_fusion.2.act_own), channel_id=1, source_target_pairs={{0,1},{1,0},{2,3},{3,2},{4,5},{5,4},{6,7},{7,6},{8,9},{9,8},{10,11... | collective-permute-start | bytes 786440 | tf_op jit(solution)/shard_map/ppermute | solution.py:55
  37.4 1.3 copy-start
  38.7 1.3 copy-start.1
  49.0 26.7 %copy-start.7 = (bf16[4,2,32,1848]{3,2,1,0:T(8,128)(2,1)S(1)}, bf16[4,2,32,1848]{3,2,1,0:T(8,128)(2,1)}, u32[]{:S(2)}) copy-start(bf16[4,2,32,1848]{3,2,1,0:T(8,128)(2,1)} %copy-done.6) | copy-start | bytes 2838532
  49.0 14.9 %collective-permute-start.6 = (bf16[4,2,32,1848]{3,2,1,0:T(8,128)(2,1)}, bf16[4,2,32,1848]{3,2,1,0:T(8,128)(2,1)}, u32[]{:S(2)}, u32[]{:S(2)}) collective-permute-start(bf16[4,2,32,1848]{3,2,1,0:T(8,128)(2,1)} %get-tuple-element.38), channel_id=1, source_target_pairs={{0,16},{1,65},{16,32},{17,81},{32,48},{33,97},{48,0},{49,113},{64,... | collective-permute-start | bytes 2838536 | tf_op jit(solution)/shard_map/ppermute | solution.py:43
  50.7 25.0 %collective-permute-start.7 = (bf16[4,2,32,1848]{3,2,1,0:T(8,128)(2,1)}, bf16[4,2,32,1848]{3,2,1,0:T(8,128)(2,1)}, u32[]{:S(2)}, u32[]{:S(2)}) collective-permute-start(bf16[4,2,32,1848]{3,2,1,0:T(8,128)(2,1)} %get-tuple-element.39), channel_id=1, source_target_pairs={{0,32},{1,129},{16,48},{17,145},{32,0},{33,161},{48,16},{49,177},{... | collective-permute-start | bytes 2838536 | tf_op jit(solution)/shard_map/ppermute | solution.py:43
  53.1 22.6 %collective-permute-start.8 = (bf16[4,2,32,1848]{3,2,1,0:T(8,128)(2,1)}, bf16[4,2,32,1848]{3,2,1,0:T(8,128)(2,1)}, u32[]{:S(2)}, u32[]{:S(2)}) collective-permute-start(bf16[4,2,32,1848]{3,2,1,0:T(8,128)(2,1)} %get-tuple-element.40), channel_id=1, source_target_pairs={{0,48},{1,193},{16,0},{17,209},{32,16},{33,225},{48,32},{49,241},{... | collective-permute-start | bytes 2838536 | tf_op jit(solution)/shard_map/ppermute | solution.py:43
  54.3 29.9 %all-to-all-start.1 = ((bf16[8,32,1848]{2,1,0:T(8,128)(2,1)}), bf16[8,32,1848]{2,1,0:T(8,128)(2,1)}, u32[]{:S(2)}, u32[]{:S(2)}) async-start(bf16[8,32,1848]{2,1,0:T(8,128)(2,1)} %add_convert_fusion), calls=%async_computation.1 | async-start | bytes 1966080 | tf_op jit(solution)/shard_map/all_to_all | solution.py:69
  78.5 13.3 %collective-permute-start.9 = (bf16[2,32,1848]{2,1,0:T(8,128)(2,1)}, bf16[2,32,1848]{2,1,0:T(8,128)(2,1)}, u32[]{:S(2)}, u32[]{:S(2)}) collective-permute-start(bf16[2,32,1848]{2,1,0:T(8,128)(2,1)} %get-tuple-element.51), channel_id=1, source_target_pairs={{0,64},{1,17},{16,80},{17,33},{32,96},{33,49},{48,112},{49,1},{64,... | collective-permute-start | bytes 709640 | tf_op jit(solution)/shard_map/ppermute | solution.py:43
  79.7 12.1 %collective-permute-start.11 = (bf16[2,32,1848]{2,1,0:T(8,128)(2,1)}, bf16[2,32,1848]{2,1,0:T(8,128)(2,1)}, u32[]{:S(2)}, u32[]{:S(2)}) collective-permute-start(bf16[2,32,1848]{2,1,0:T(8,128)(2,1)} %get-tuple-element.52), channel_id=1, source_target_pairs={{0,192},{1,49},{16,208},{17,1},{32,224},{33,17},{48,240},{49,33},{... | collective-permute-start | bytes 709640 | tf_op jit(solution)/shard_map/ppermute | solution.py:43
  81.2 10.6 %collective-permute-start.10 = (bf16[2,32,1848]{2,1,0:T(8,128)(2,1)}, bf16[2,32,1848]{2,1,0:T(8,128)(2,1)}, u32[]{:S(2)}, u32[]{:S(2)}) collective-permute-start(bf16[2,32,1848]{2,1,0:T(8,128)(2,1)} %get-tuple-element.53), channel_id=1, source_target_pairs={{0,128},{1,33},{16,144},{17,49},{32,160},{33,1},{48,176},{49,17},{... | collective-permute-start | bytes 709640 | tf_op jit(solution)/shard_map/ppermute | solution.py:43
  86.2 7.8 %collective-permute-start.5 = (bf16[32,1848]{1,0:T(8,128)(2,1)}, bf16[32,1848]{1,0:T(8,128)(2,1)S(1)}, u32[]{:S(2)}, u32[]{:S(2)}) collective-permute-start(bf16[32,1848]{1,0:T(8,128)(2,1)} %reduce_sum.12), channel_id=1, source_target_pairs={{0,0},{1,16},{2,32},{3,48},{4,64},{5,80},{6,96},{7,112},{8,128},{9... | collective-permute-start | bytes 354824 | tf_op jit(solution)/shard_map/ppermute | solution.py:60
  94.2 16.7 %collective-permute-start.13 = (bf16[2,32,1848]{2,1,0:T(8,128)(2,1)S(1)}, bf16[2,32,1848]{2,1,0:T(8,128)(2,1)S(1)}, u32[]{:S(2)}, u32[]{:S(2)}) collective-permute-start(bf16[2,32,1848]{2,1,0:T(8,128)(2,1)S(1)} %get-tuple-element.64), channel_id=1, source_target_pairs={{0,128},{1,33},{16,144},{17,49},{32,160},{33,1},{48,176},{49,17},{... | collective-permute-start | bytes 709640 | tf_op jit(solution)/shard_map/ppermute | solution.py:43
  104.6 9.4 %collective-permute-start.12 = (bf16[2,32,1848]{2,1,0:T(8,128)(2,1)S(1)}, bf16[2,32,1848]{2,1,0:T(8,128)(2,1)S(1)}, u32[]{:S(2)}, u32[]{:S(2)}) collective-permute-start(bf16[2,32,1848]{2,1,0:T(8,128)(2,1)S(1)} %get-tuple-element.64), channel_id=1, source_target_pairs={{0,192},{1,49},{16,208},{17,1},{32,224},{33,17},{48,240},{49,33},{... | collective-permute-start | bytes 709640 | tf_op jit(solution)/shard_map/ppermute | solution.py:43
  107.0 7.0 %collective-permute-start.14 = (bf16[2,32,1848]{2,1,0:T(8,128)(2,1)S(1)}, bf16[2,32,1848]{2,1,0:T(8,128)(2,1)S(1)}, u32[]{:S(2)}, u32[]{:S(2)}) collective-permute-start(bf16[2,32,1848]{2,1,0:T(8,128)(2,1)S(1)} %get-tuple-element.64), channel_id=1, source_target_pairs={{0,64},{1,17},{16,80},{17,33},{32,96},{33,49},{48,112},{49,1},{64,... | collective-permute-start | bytes 709640 | tf_op jit(solution)/shard_map/ppermute | solution.py:43
  107.5 8.0 %collective-permute-start.15 = (bf16[32,1848]{1,0:T(8,128)(2,1)S(1)}, bf16[32,1848]{1,0:T(8,128)(2,1)S(1)}, u32[]{:S(2)}, u32[]{:S(2)}) collective-permute-start(bf16[32,1848]{1,0:T(8,128)(2,1)S(1)} %get-tuple-element.60), channel_id=1, source_target_pairs={{0,0},{1,17},{2,34},{3,51},{4,68},{5,85},{6,102},{7,119},{8,136},{... | collective-permute-start | bytes 354824 | tf_op jit(solution)/shard_map/ppermute | solution.py:65
  116.6 39.2 %all-to-all-start.2 = ((bf16[8,32,1848]{2,1,0:T(8,128)(2,1)}), bf16[8,32,1848]{2,1,0:T(8,128)(2,1)S(1)}, u32[]{:S(2)}, u32[]{:S(2)}) async-start(bf16[8,32,1848]{2,1,0:T(8,128)(2,1)} %broadcast_in_dim.8), calls=%async_computation.2 | async-start | bytes 1966080 | tf_op jit(solution)/shard_map/all_to_all | solution.py:69
  128.0 28.3 %collective-permute-start.18 = (bf16[4,2,32,1848]{3,2,1,0:T(8,128)(2,1)}, bf16[4,2,32,1848]{3,2,1,0:T(8,128)(2,1)}, u32[]{:S(2)}, u32[]{:S(2)}) collective-permute-start(bf16[4,2,32,1848]{3,2,1,0:T(8,128)(2,1)} %pad_maximum_fusion.g0), channel_id=1, source_target_pairs={{0,16},{1,65},{16,32},{17,81},{32,48},{33,97},{48,0},{49,113},{64,... | collective-permute-start | bytes 2838536 | tf_op jit(solution)/shard_map/ppermute | solution.py:43
  128.2 28.2 %collective-permute-start.17 = (bf16[4,2,32,1848]{3,2,1,0:T(8,128)(2,1)}, bf16[4,2,32,1848]{3,2,1,0:T(8,128)(2,1)}, u32[]{:S(2)}, u32[]{:S(2)}) collective-permute-start(bf16[4,2,32,1848]{3,2,1,0:T(8,128)(2,1)} %pad_maximum_fusion.g0), channel_id=1, source_target_pairs={{0,32},{1,129},{16,48},{17,145},{32,0},{33,161},{48,16},{49,177},{... | collective-permute-start | bytes 2838536 | tf_op jit(solution)/shard_map/ppermute | solution.py:43
  128.9 27.5 %collective-permute-start.16 = (bf16[4,2,32,1848]{3,2,1,0:T(8,128)(2,1)}, bf16[4,2,32,1848]{3,2,1,0:T(8,128)(2,1)}, u32[]{:S(2)}, u32[]{:S(2)}) collective-permute-start(bf16[4,2,32,1848]{3,2,1,0:T(8,128)(2,1)} %pad_maximum_fusion.g0), channel_id=1, source_target_pairs={{0,48},{1,193},{16,0},{17,209},{32,16},{33,225},{48,32},{49,241},{... | collective-permute-start | bytes 2838536 | tf_op jit(solution)/shard_map/ppermute | solution.py:43
  155.8 18.8 %collective-permute-start.19 = (bf16[8,32,1848]{2,1,0:T(8,128)(2,1)S(1)}, bf16[8,32,1848]{2,1,0:T(8,128)(2,1)}, u32[]{:S(2)}, u32[]{:S(2)}) collective-permute-start(bf16[8,32,1848]{2,1,0:T(8,128)(2,1)S(1)} %all-to-all-done.2.hid_own), channel_id=1, source_target_pairs={{0,1},{1,0},{2,3},{3,2},{4,5},{5,4},{6,7},{7,6},{8,9},{9,8},{10,11... | collective-permute-start | bytes 2838536 | tf_op jit(solution)/shard_map/ppermute | solution.py:55
  173.3 1.4 copy-start.13
  173.3 1.4 copy-start.19
  179.0 3.0 %collective-permute-start.20 = (f32[174,8,128]{2,1,0:T(8,128)S(1)}, f32[174,8,128]{2,1,0:T(8,128)S(1)}, u32[]{:S(2)}, u32[]{:S(2)}) collective-permute-start(f32[174,8,128]{2,1,0:T(8,128)S(1)} %pad_maximum_fusion.1), channel_id=1, source_target_pairs={{0,1},{1,0},{2,3},{3,2},{4,5},{5,4},{6,7},{7,6},{8,9},{9,8},{10,11... | collective-permute-start | bytes 2138120 | tf_op jit(solution)/shard_map/ppermute | solution.py:55
  179.2 10.0 %collective-permute-start.27 = (bf16[136,8,128]{2,1,0:T(8,128)(2,1)S(1)}, bf16[136,8,128]{2,1,0:T(8,128)(2,1)S(1)}, u32[]{:S(2)}, u32[]{:S(2)}) collective-permute-start(bf16[136,8,128]{2,1,0:T(8,128)(2,1)S(1)} %convert_element_type.180), channel_id=1, source_target_pairs={{0,16},{1,65},{16,32},{17,81},{32,48},{33,97},{48,0},{49,113},{64,... | collective-permute-start | bytes 835592 | tf_op jit(solution)/shard_map/ppermute | solution.py:43
  179.4 9.8 %collective-permute-start.26 = (bf16[136,8,128]{2,1,0:T(8,128)(2,1)S(1)}, bf16[136,8,128]{2,1,0:T(8,128)(2,1)S(1)}, u32[]{:S(2)}, u32[]{:S(2)}) collective-permute-start(bf16[136,8,128]{2,1,0:T(8,128)(2,1)S(1)} %convert_element_type.180), channel_id=1, source_target_pairs={{0,32},{1,129},{16,48},{17,145},{32,0},{33,161},{48,16},{49,177},{... | collective-permute-start | bytes 835592 | tf_op jit(solution)/shard_map/ppermute | solution.py:43
  181.6 8.2 %collective-permute-start.25 = (bf16[136,8,128]{2,1,0:T(8,128)(2,1)S(1)}, bf16[136,8,128]{2,1,0:T(8,128)(2,1)S(1)}, u32[]{:S(2)}, u32[]{:S(2)}) collective-permute-start(bf16[136,8,128]{2,1,0:T(8,128)(2,1)S(1)} %convert_element_type.180), channel_id=1, source_target_pairs={{0,48},{1,193},{16,0},{17,209},{32,16},{33,225},{48,32},{49,241},{... | collective-permute-start | bytes 835592 | tf_op jit(solution)/shard_map/ppermute | solution.py:43
  182.1 12.5 %collective-permute-start.21 = (bf16[110,8,128]{2,1,0:T(8,128)(2,1)S(1)}, bf16[110,8,128]{2,1,0:T(8,128)(2,1)S(1)}, u32[]{:S(2)}, u32[]{:S(2)}) collective-permute-start(bf16[110,8,128]{2,1,0:T(8,128)(2,1)S(1)} %pad_maximum_fusion.5), channel_id=1, source_target_pairs={{0,2},{2,0},{4,6},{6,4},{8,10},{10,8},{12,14},{14,12},{1,3},{3,1},... | collective-permute-start | bytes 675848 | tf_op jit(solution)/shard_map/ppermute | solution.py:51
  189.9 7.6 %collective-permute-start.30 = (bf16[136,8,128]{2,1,0:T(8,128)(2,1)S(1)}, bf16[136,8,128]{2,1,0:T(8,128)(2,1)S(1)}, u32[]{:S(2)}, u32[]{:S(2)}) collective-permute-start(bf16[136,8,128]{2,1,0:T(8,128)(2,1)S(1)} %fusion.14), channel_id=1, source_target_pairs={{0,64},{1,17},{16,80},{17,33},{32,96},{33,49},{48,112},{49,1},{64,... | collective-permute-start | bytes 835592 | tf_op jit(solution)/shard_map/ppermute | solution.py:43
  191.5 9.5 %collective-permute-start.29 = (bf16[136,8,128]{2,1,0:T(8,128)(2,1)S(1)}, bf16[136,8,128]{2,1,0:T(8,128)(2,1)S(1)}, u32[]{:S(2)}, u32[]{:S(2)}) collective-permute-start(bf16[136,8,128]{2,1,0:T(8,128)(2,1)S(1)} %fusion.14), channel_id=1, source_target_pairs={{0,128},{1,33},{16,144},{17,49},{32,160},{33,1},{48,176},{49,17},{... | collective-permute-start | bytes 835592 | tf_op jit(solution)/shard_map/ppermute | solution.py:43
  193.8 7.2 %collective-permute-start.28 = (bf16[136,8,128]{2,1,0:T(8,128)(2,1)S(1)}, bf16[136,8,128]{2,1,0:T(8,128)(2,1)S(1)}, u32[]{:S(2)}, u32[]{:S(2)}) collective-permute-start(bf16[136,8,128]{2,1,0:T(8,128)(2,1)S(1)} %fusion.14), channel_id=1, source_target_pairs={{0,192},{1,49},{16,208},{17,1},{32,224},{33,17},{48,240},{49,33},{... | collective-permute-start | bytes 835592 | tf_op jit(solution)/shard_map/ppermute | solution.py:43
  194.8 10.2 %collective-permute-start.22 = (bf16[78,8,128]{2,1,0:T(8,128)(2,1)S(1)}, bf16[78,8,128]{2,1,0:T(8,128)(2,1)S(1)}, u32[]{:S(2)}, u32[]{:S(2)}) collective-permute-start(bf16[78,8,128]{2,1,0:T(8,128)(2,1)S(1)} %pad_maximum_fusion.7), channel_id=1, source_target_pairs={{0,4},{2,6},{4,0},{6,2},{8,12},{10,14},{12,8},{14,10},{1,5},{3,7},... | collective-permute-start | bytes 479240 | tf_op jit(solution)/shard_map/ppermute | solution.py:51
  205.1 9.0 %collective-permute-start.23 = (bf16[62,8,128]{2,1,0:T(8,128)(2,1)S(1)}, bf16[62,8,128]{2,1,0:T(8,128)(2,1)S(1)}, u32[]{:S(2)}, u32[]{:S(2)}) collective-permute-start(bf16[62,8,128]{2,1,0:T(8,128)(2,1)S(1)} %pad_maximum_fusion.9), channel_id=1, source_target_pairs={{0,8},{2,10},{4,12},{6,14},{8,0},{10,2},{12,4},{14,6},{1,9},{3,11}... | collective-permute-start | bytes 380936 | tf_op jit(solution)/shard_map/ppermute | solution.py:51
  214.2 5.3 %collective-permute-start.24 = (f32[46,8,128]{2,1,0:T(8,128)S(1)}, f32[46,8,128]{2,1,0:T(8,128)S(1)}, u32[]{:S(2)}, u32[]{:S(2)}) collective-permute-start(f32[46,8,128]{2,1,0:T(8,128)S(1)} %slice_add_fusion.2), channel_id=1, source_target_pairs={{0,1},{1,0},{2,3},{3,2},{4,5},{5,4},{6,7},{7,6},{8,9},{9,8},{10,11... | collective-permute-start | bytes 565256 | tf_op jit(solution)/shard_map/ppermute | solution.py:55
  (7 other events, 6.9 us)
where the time goes:
time: 222 us; the launch traced here: 221 us
  starting transfers between devices  91.5 us (41%)
  waiting for transfers between devices  67.6 us (30%)
  Pallas kernels  29.3 us (13%)
  local copies, waits for them, and re-layouts  18.4 us (8%)
  other arithmetic  13 us (6%)
    ppermute x18, starting transfers between devices, plane_permute(): return lax.ppermute(v, ('y', 'x', 'core'), perm)  32.6 us
    ppermute x18, waiting for transfers between devices, plane_permute(): return lax.ppermute(v, ('y', 'x', 'core'), perm)  29.9 us
    pallas_call x6, Pallas kernels, kernel_call(): pl.pallas_call(body, out_shape=[jax.ShapeDtypeStruct(s, d) for s, d in ou...  29.3 us
    all_to_all x3, waiting for transfers between devices, to_all(): return lax.all_to_all(v, axis, split_axis=0, concat_axis=0, tiled=True)  26.9 us
    all_to_all x3, starting transfers between devices, to_all(): return lax.all_to_all(v, axis, split_axis=0, concat_axis=0, tiled=True)  22.5 us
    ppermute x6, starting transfers between devices, z_swap(): return lax.ppermute(v, 'z', [(i, i ^ mask) for i in range(NZ)])  19.5 us
    unnamed x43, local copies, waits for them, and re-layouts  12.3 us
    ppermute x6, waiting for transfers between devices, z_swap(): return lax.ppermute(v, 'z', [(i, i ^ mask) for i in range(NZ)])  9.63 us
  transfers between devices with their start and end apart: 34, of which 15 were waited for; matrix products, arithmetic and copies ran while one was open for 7% of the time, Pallas kernels for 8%

commit v1 on v0

--- a/solution.py
+++ b/solution.py
@@ -12,7 +12,7 @@
 COL = ("z", "core")
 TILE = 256
 LANES = 128
-VMEM_LIMIT = 48 * 1024 * 1024
+MIB = 1024 * 1024
 BITREV = (0, 4, 2, 6, 1, 5, 3, 7)
 
 
@@ -20,14 +20,15 @@
     return [(at, min(at + TILE, width)) for at in range(0, width, TILE)]
 
 
-def kernel_call(body, ids, args, outs, scratch=()):
+def kernel_call(body, ids, args, outs, scratch=(), raw=0, limit=32):
     return pl.pallas_call(
         body,
         out_shape=[jax.ShapeDtypeStruct(s, d) for s, d in outs],
-        in_specs=[pl.BlockSpec(memory_space=pltpu.SMEM)] + [pl.BlockSpec(memory_space=pltpu.VMEM)] * len(args),
+        in_specs=[pl.BlockSpec(memory_space=pltpu.SMEM)] + [pl.BlockSpec(memory_space=pl.ANY)] * raw
+        + [pl.BlockSpec(memory_space=pltpu.VMEM)] * (len(args) - raw),
         out_specs=[pl.BlockSpec(memory_space=pltpu.VMEM)] * len(outs),
         scratch_shapes=list(scratch),
-        compiler_params=pltpu.CompilerParams(vmem_limit_bytes=VMEM_LIMIT),
+        compiler_params=pltpu.CompilerParams(vmem_limit_bytes=limit * MIB),
         cost_estimate=pl.CostEstimate(flops=1024, bytes_accessed=1024, transcendentals=0),
     )(ids, *args)
 
@@ -55,14 +56,36 @@
     return lax.ppermute(v, "core", [(0, 1), (1, 0)])
 
 
+MOVES = (
+    (3, 2), (2, 2), (2, 0), (2, 1), (1, 1), (3, 3), (0, 3), (1, 0),
+    (0, 0), (0, 1), (3, 0), (0, 2), (1, 3), (3, 1), (2, 3), (1, 2),
+)
+
+
+def grid_pairs():
+    pairs = []
+    for j in range(16):
+        for b in range(16):
+            oy, ox = MOVES[(b - (j & 14)) & 15]
+            a = (((j >> 2) + oy) & 3) * 4 + (((j & 3) + ox) & 3)
+            pairs.append((j * 16 + b, a * 16 + j))
+    return pairs
+
+
 def to_columns(v):
-    perm = [(j * 16 + b, (b ^ j) * 16 + j) for j in range(16) for b in range(16)]
-    return lax.ppermute(v, ("y", "x", "z", "core"), perm)
+    return lax.ppermute(v, ("y", "x", "z", "core"), grid_pairs())
 
 
 def to_rows(v):
-    perm = [(a * 16 + j, j * 16 + (a ^ j)) for a in range(16) for j in range(16)]
-    return lax.ppermute(v, ("y", "x", "z", "core"), perm)
+    return lax.ppermute(v, ("y", "x", "z", "core"), [(b, a) for a, b in grid_pairs()])
+
+
+def move_table():
+    words = [0, 0]
+    for source, (oy, ox) in enumerate(MOVES):
+        at = oy * 4 + ox
+        words[at // 8] |= source << (4 * (at % 8))
+    return [w - (1 << 32) if w >= 1 << 31 else w for w in words]
 
 
 def to_all(v, axis):
@@ -111,7 +134,12 @@
     one, two = at // 4, at % 4
     dx = jnp.where(core == 0, one, two)
     dy = jnp.where(core == 0, two, one)
-    return (((y + dy) & 3) * 4 + ((x + dx) & 3)) ^ (z * 2 + core)
+    unit = z * 2 + core
+    oy, ox = (y + dy - (unit >> 2)) & 3, (x + dx - (unit & 3)) & 3
+    low, high = move_table()
+    word = jnp.where(oy < 2, jnp.int32(low), jnp.int32(high))
+    source = lax.shift_right_logical(word, ((oy & 1) * 4 + ox) * 4) & 15
+    return ((z * 2 + (source & 14)) & 15) | (source & 1)
 
 
 def slot_of(off):
@@ -174,28 +202,39 @@
     return v.swapaxes(1, 2).reshape(32, blocks * LANES)[:, :width]
 
 
-def grad_body(ids, g0, g1, g2, g3, rel, *refs):
-    bases, effs, wides, narrows = refs[0:2], refs[2:4], refs[4:6], refs[6:8]
-    gi, left, right, acc = refs[8:]
-    a = rel[...]
-    dm = rel.shape[1]
+def grad_body(ids, gate_base, gate_eff, up_base, up_eff, g0, g1, g2, g3, rel, *refs):
+    wides, narrows = refs[0:2], refs[2:4]
+    gi, left, right, acc, weights, sems = refs[4:]
+    copies = [
+        pltpu.make_async_copy(src, weights.at[k], sems.at[k])
+        for k, src in enumerate((gate_eff, up_eff, gate_base, up_base))
+    ]
+    for copy in copies:
+        copy.start()
+    width, dm = weights.shape[1:]
+    blocks = -(-width // LANES)
+
+    def tile(m, lo, hi):
+        return jnp.concatenate([r[:, m, :, lo:hi].reshape(128, hi - lo) for r in (g0, g1, g2, g3)], axis=0)
+
     for m in range(2):
-        base, eff, wide, narrow = bases[m], effs[m], wides[m], narrows[m]
-        width = base.shape[0]
-        blocks = -(-width // LANES)
-        n2 = hilo(narrow[...])
-        total = jnp.zeros((64, dm), F32)
+        copies[m].wait()
         for n, (lo, hi) in enumerate(tiles(width)):
-            g = jnp.concatenate([r[:, m, :, lo:hi].reshape(128, hi - lo) for r in (g0, g1, g2, g3)], axis=0)
-            term = nn(g, eff[lo:hi, :])
-            masked = (tn(g, a) * base[lo:hi, :].astype(F32)).astype(BF16)
-            rp = nt(n2, masked)
-            total = total + nn(hilo(wide[:, lo:hi]), masked)
-            store_tiles(right, m * 4 * blocks, blocks, lo, rp[:32] + rp[32:])
+            term = nn(tile(m, lo, hi), weights[m, lo:hi, :])
             if n == 0 and m == 0:
                 acc[...] = term
             else:
                 acc[...] += term
+    a = rel[...]
+    for m in range(2):
+        copies[2 + m].wait()
+        n2 = hilo(narrows[m][...])
+        total = jnp.zeros((64, dm), F32)
+        for lo, hi in tiles(width):
+            masked = (tn(tile(m, lo, hi), a) * weights[2 + m, lo:hi, :].astype(F32)).astype(BF16)
+            rp = nt(n2, masked)
+            total = total + nn(hilo(wides[m][:, lo:hi]), masked)
+            store_tiles(right, m * 4 * blocks, blocks, lo, rp[:32] + rp[32:])
         store_tiles(left, m * dm // 32, dm // LANES, 0, total[:32] + total[32:])
     z, core = ids[2], ids[3]
     for at in range(16):
@@ -283,8 +322,8 @@
     grad_h = to_columns(grad_h.astype(BF16)).astype(F32)
 
     got = scatter4(chunks, True)
-    parts = [add_all(*[g[k] for g in got]) for k in range(4)]
-    zs = add_all(*scatter4([parts[0]] + [p.astype(BF16) for p in parts[1:]], False))
+    parts = [add_all(*[g[k] for g in got]).astype(BF16) for k in range(4)]
+    zs = add_all(*scatter4(parts, False))
 
     hidden, d_gate, d_up = swish_parts(zs[0], zs[1], grad_h)
     hid = to_rows(hidden)
@@ -298,13 +337,15 @@
     gi, l_up, r_up = kernel_call(
         grad_body,
         ids,
-        [*grads, act_rel, gate_t, up_t, gate_eff, up_eff, gate_right, up_right, gate_left, up_left],
+        [gate_t, gate_eff, up_t, up_eff, *grads, act_rel, gate_right, up_right, gate_left, up_left],
         [
             ((2, 8, narrow_tiles, 8, LANES), F32),
             ((2 * narrow_tiles, 8, LANES), F32),
             ((2 * wide_tiles, 8, LANES), F32),
         ],
-        scratch=[pltpu.VMEM((512, dm), F32)],
+        scratch=[pltpu.VMEM((512, dm), F32), pltpu.VMEM((4, ff, dm), BF16), pltpu.SemaphoreType.DMA((4,))],
+        raw=4,
+        limit=60,
     )
     l_down, r_down = kernel_call(
         down_grad_body,
@@ -312,6 +353,7 @@
         [hid_own, hid_other, cot, down_base, down_left, down_right],
         [((wide_tiles, 8, LANES), F32), ((narrow_tiles, 8, LANES), F32)],
         scratch=[pltpu.VMEM((512, dm), BF16)],
+        limit=60,
     )
 
     r_all = jnp.concatenate([r_up, r_down], axis=0)

time: 222 us -> 210 us (0.946)
  starting transfers between devices: 91.5 us -> 71.1 us
  waiting for transfers between devices: 67.6 us -> 83.2 us
  local copies, waits for them, and re-layouts: 18.4 us -> 13.2 us
    ppermute x2, waiting for transfers between devices: 0.77 us -> 14.8 us  [the longest x1 8.17 us: to_columns(): return lax.ppermute(v, ('y', 'x', 'z', 'core'), grid_pairs())]
    ppermute x18, starting transfers between devices: 32.6 us -> 20.3 us  [plane_permute(): return lax.ppermute(v, ('y', 'x', 'core'), perm)]
    all_to_all x3, starting transfers between devices: 22.5 us -> 14.1 us  [to_all(): return lax.all_to_all(v, axis, split_axis=0, concat_axis=0, tiled=True)]
    unnamed x43 -> x49, local copies, waits for them, and re-layouts: 12.3 us -> 7.14 us
  transfers between devices with their start and end apart: 34 -> 34, of which waited for: 15 -> 19; matrix products, arithmetic and copies ran while one was open for 7% -> 7% of each run, Pallas kernels for 8% -> 8%
where the time goes in v1:
time: 210 us; the launch traced here: 209 us
  waiting for transfers between devices  83.2 us (40%)
  starting transfers between devices  71.1 us (34%)
  Pallas kernels  28.4 us (14%)
  local copies, waits for them, and re-layouts  13.2 us (6%)
  other arithmetic  11.8 us (6%)
    ppermute x18, waiting for transfers between devices, plane_permute(): return lax.ppermute(v, ('y', 'x', 'core'), perm)  31.4 us
    all_to_all x3, waiting for transfers between devices, to_all(): return lax.all_to_all(v, axis, split_axis=0, concat_axis=0, tiled=True)  28.4 us
    pallas_call x6, Pallas kernels, kernel_call(): pl.pallas_call(body, out_shape=[jax.ShapeDtypeStruct(s, d) for s, d in ou...  28.4 us
    ppermute x18, starting transfers between devices, plane_permute(): return lax.ppermute(v, ('y', 'x', 'core'), perm)  20.3 us
    ppermute x6, starting transfers between devices, z_swap(): return lax.ppermute(v, 'z', [(i, i ^ mask) for i in range(NZ)])  20 us
    all_to_all x3, starting transfers between devices, to_all(): return lax.all_to_all(v, axis, split_axis=0, concat_axis=0, tiled=True)  14.1 us
    ppermute x5, starting transfers between devices, core_swap(): return lax.ppermute(v, 'core', [(0, 1), (1, 0)])  8.81 us
    ppermute x1, waiting for transfers between devices, to_columns(): return lax.ppermute(v, ('y', 'x', 'z', 'core'), grid_pairs())  8.17 us
  transfers between devices with their start and end apart: 34, of which 19 were waited for; matrix products, arithmetic and copies ran while one was open for 7% of the time, Pallas kernels for 8%

profile of v1, /device:TPU:1, one launch (start us, length us, event | category | flops | bytes accessed | tf_op | source)
XLA Modules:
  0.0 208.8 jit_solution(1751718674539199503)
XLA Ops:
  0.7 7.8 %collective-permute-start = (bf16[1,32,512]{2,1,0:T(8,128)(2,1)}, bf16[1,32,512]{2,1,0:T(8,128)(2,1)S(1)}, u32[]{:S(2)}, u32[]{:S(2)}) collective-permute-start(bf16[1,32,512]{2,1,0:T(8,128)(2,1)} %bitcast.93), channel_id=1, source_target_pairs={{0,8},{2,10},{4,12},{6,14},{8,0},{10,2},{12,4},{14,6},{1,9},{3,11}... | collective-permute-start | bytes 98312 | tf_op jit(solution)/shard_map/ppermute | solution.py:52
  8.5 1.6 broadcast_in_dim.7
  10.1 6.8 %all-to-all-start = ((bf16[16,32,512]{2,1,0:T(8,128)(2,1)}), bf16[16,32,512]{2,1,0:T(8,128)(2,1)S(1)}, u32[]{:S(2)}, u32[]{:S(2)}) async-start(bf16[16,32,512]{2,1,0:T(8,128)(2,1)} %broadcast_in_dim.7), calls=%async_computation | async-start | bytes 1048576 | tf_op jit(solution)/shard_map/all_to_all | solution.py:92
  17.6 1.2 collective-permute-start.1
  18.8 3.8 %collective-permute-done.1 = bf16[2,32,512]{2,1,0:T(8,128)(2,1)S(1)} collective-permute-done((bf16[2,32,512]{2,1,0:T(8,128)(2,1)S(1)}, bf16[2,32,512]{2,1,0:T(8,128)(2,1)S(1)}, u32[]{:S(2)}, u32[]{:S(2)}) %collective-permute-start.1) | collective-permute-done | bytes 65568 | tf_op jit(solution)/shard_map/ppermute | solution.py:52
  24.6 1.2 shard_map.163.eff
  25.8 1.3 copy-done.5
  28.6 1.5 copy-done.6
  30.1 1.8 shard_map.164
  32.0 3.1 %collective-permute-start.4 = (bf16[8,32,1848]{2,1,0:T(8,128)(2,1)S(1)}, bf16[8,32,1848]{2,1,0:T(8,128)(2,1)S(1)}, u32[]{:S(2)}, u32[]{:S(2)}) collective-permute-start(bf16[8,32,1848]{2,1,0:T(8,128)(2,1)S(1)} %get-tuple-element.33), channel_id=1, source_target_pairs={{0,1},{1,0},{2,3},{3,2},{4,5},{5,4},{6,7},{7,6},{8,9},{9,8},{10,11... | collective-permute-start | bytes 2838536 | tf_op jit(solution)/shard_map/ppermute | solution.py:56
  35.2 1.5 copy-done.1
  36.7 1.7 shard_map.162
  38.5 1.4 add_convert_fusion
  39.9 4.2 %shard_map.165 = (bf16[4,2,32,1848]{3,2,1,0:T(8,128)(2,1)S(1)}, bf16[4,2,32,1848]{3,2,1,0:T(8,128)(2,1)}, bf16[4,2,32,1848]{3,2,1,0:T(8,128)(2,1)}, bf16[4,2,32,...) custom-call(s32[4]{0:T(128)S(1)} %pad_add_fusion.ids, bf16[8,32,512]{2,1,0:T(8,128)(2,1)S(1)} %pad_maximum_fusion.2.act_own, ...), custom_call_target="tpu_custom_call" | custom-call | flops 1024 | bytes 1024 | tf_op jit(solution)/shard_map/pallas_call | solution.py:24
  44.8 1.6 collective-permute-start.6
  46.5 2.4 %collective-permute-start.7 = (bf16[4,2,32,1848]{3,2,1,0:T(8,128)(2,1)}, bf16[4,2,32,1848]{3,2,1,0:T(8,128)(2,1)}, u32[]{:S(2)}, u32[]{:S(2)}) collective-permute-start(bf16[4,2,32,1848]{3,2,1,0:T(8,128)(2,1)} %get-tuple-element.39), channel_id=1, source_target_pairs={{0,32},{1,129},{16,48},{17,145},{32,0},{33,161},{48,16},{49,177},{... | collective-permute-start | bytes 2838536 | tf_op jit(solution)/shard_map/ppermute | solution.py:44
  48.9 1.2 collective-permute-start.8
  50.1 3.6 %all-to-all-start.1 = ((bf16[8,32,1848]{2,1,0:T(8,128)(2,1)}), bf16[8,32,1848]{2,1,0:T(8,128)(2,1)S(1)}, u32[]{:S(2)}, u32[]{:S(2)}) async-start(bf16[8,32,1848]{2,1,0:T(8,128)(2,1)} %add_convert_fusion), calls=%async_computation.1 | async-start | bytes 1966080 | tf_op jit(solution)/shard_map/all_to_all | solution.py:92
  53.6 6.2 %collective-permute-done.6 = bf16[4,2,32,1848]{3,2,1,0:T(8,128)(2,1)} collective-permute-done((bf16[4,2,32,1848]{3,2,1,0:T(8,128)(2,1)}, bf16[4,2,32,1848]{3,2,1,0:T(8,128)(2,1)}, u32[]{:S(2)}, u32[]{:S(2)}) %collective-permute-start.6) | collective-permute-done | bytes 946208 | tf_op jit(solution)/shard_map/ppermute | solution.py:44
  59.8 11.7 %collective-permute-done.7 = bf16[4,2,32,1848]{3,2,1,0:T(8,128)(2,1)} collective-permute-done((bf16[4,2,32,1848]{3,2,1,0:T(8,128)(2,1)}, bf16[4,2,32,1848]{3,2,1,0:T(8,128)(2,1)}, u32[]{:S(2)}, u32[]{:S(2)}) %collective-permute-start.7) | collective-permute-done | bytes 946208 | tf_op jit(solution)/shard_map/ppermute | solution.py:44
  71.5 2.0 fusion.7
  73.6 1.2 collective-permute-start.9
  74.7 1.6 collective-permute-start.11
  76.3 1.2 collective-permute-start.10
  77.5 3.8 %all-to-all-done.1 = bf16[8,32,1848]{2,1,0:T(8,128)(2,1)S(1)} async-done(((bf16[8,32,1848]{2,1,0:T(8,128)(2,1)}), bf16[8,32,1848]{2,1,0:T(8,128)(2,1)S(1)}, u32[]{:S(2)}, u32[]{:S(2)}) %all-to-all-start.1) | async-done | bytes 946208 | tf_op jit(solution)/shard_map/all_to_all | solution.py:92
  82.1 3.1 %collective-permute-start.5 = (bf16[32,1848]{1,0:T(8,128)(2,1)}, bf16[32,1848]{1,0:T(8,128)(2,1)S(1)}, u32[]{:S(2)}, u32[]{:S(2)}) collective-permute-start(bf16[32,1848]{1,0:T(8,128)(2,1)} %reduce_sum.12), channel_id=1, source_target_pairs={{0,224},{1,160},{2,128},{3,144},{4,80},{5,240},{6,48},{7,64},{8,0}... | collective-permute-start | bytes 354824 | tf_op jit(solution)/shard_map/ppermute | solution.py:76
  85.2 1.4 fusion.1
  86.6 8.2 %collective-permute-done.5 = bf16[32,1848]{1,0:T(8,128)(2,1)S(1)} collective-permute-done((bf16[32,1848]{1,0:T(8,128)(2,1)}, bf16[32,1848]{1,0:T(8,128)(2,1)S(1)}, u32[]{:S(2)}, u32[]{:S(2)}) %collective-permute-start.5) | collective-permute-done | bytes 118304 | tf_op jit(solution)/shard_map/ppermute | solution.py:76
  95.1 1.1 collective-permute-start.12
  96.6 4.7 %collective-permute-start.15 = (bf16[32,1848]{1,0:T(8,128)(2,1)S(1)}, bf16[32,1848]{1,0:T(8,128)(2,1)S(1)}, u32[]{:S(2)}, u32[]{:S(2)}) collective-permute-start(bf16[32,1848]{1,0:T(8,128)(2,1)S(1)} %get-tuple-element.60), channel_id=1, source_target_pairs={{224,0},{160,1},{128,2},{144,3},{80,4},{240,5},{48,6},{64,7},{0,8}... | collective-permute-start | bytes 354824 | tf_op jit(solution)/shard_map/ppermute | solution.py:80
  101.9 1.7 collective-permute-done.12
  104.7 6.6 %collective-permute-done.15 = bf16[32,1848]{1,0:T(8,128)(2,1)S(1)} collective-permute-done((bf16[32,1848]{1,0:T(8,128)(2,1)S(1)}, bf16[32,1848]{1,0:T(8,128)(2,1)S(1)}, u32[]{:S(2)}, u32[]{:S(2)}) %collective-permute-start.15) | collective-permute-done | bytes 118304 | tf_op jit(solution)/shard_map/ppermute | solution.py:80
  112.4 3.8 %all-to-all-start.2 = ((bf16[8,32,1848]{2,1,0:T(8,128)(2,1)}), bf16[8,32,1848]{2,1,0:T(8,128)(2,1)S(1)}, u32[]{:S(2)}, u32[]{:S(2)}) async-start(bf16[8,32,1848]{2,1,0:T(8,128)(2,1)} %broadcast_in_dim.8), calls=%async_computation.2 | async-start | bytes 1966080 | tf_op jit(solution)/shard_map/all_to_all | solution.py:92
  117.4 2.0 collective-permute-start.16
  119.4 24.6 %all-to-all-done.2.hid_own = bf16[8,32,1848]{2,1,0:T(8,128)(2,1)S(1)} async-done(((bf16[8,32,1848]{2,1,0:T(8,128)(2,1)}), bf16[8,32,1848]{2,1,0:T(8,128)(2,1)S(1)}, u32[]{:S(2)}, u32[]{:S(2)}) %all-to-all-start.2) | async-done | bytes 946208 | tf_op jit(solution)/shard_map/all_to_all | solution.py:92
  144.5 13.6 %shard_map.166 = (f32[2,8,16,8,128]{4,3,2,1,0:T(8,128)}, f32[32,8,128]{2,1,0:T(8,128)}, f32[120,8,128]{2,1,0:T(8,128)}) custom-call(s32[4]{0:T(128)} %copy-done.15, bf16[1848,512]{1,0:T(8,128)(2,1)} %bitcast.88, bf16[1848,512]{1,0:T(8,128)(2,1)} %copy-done.2, bf16[1848,512]{1,0:T(8,128)(2,1)} %bitcast.90, bf16[1848,512]{1,0:T(8,128)(2,1)} %copy-done.3, ...), custom_call_target="tpu_custom_call" | custom-call | flops 1024 | bytes 1024 | tf_op jit(solution)/shard_map/pallas_call | solution.py:24
  158.1 1.3 fusion.19
  160.4 5.9 %shard_map.167 = (f32[60,8,128]{2,1,0:T(8,128)}, f32[16,8,128]{2,1,0:T(8,128)}) custom-call(s32[4]{0:T(128)} %copy-done.15, bf16[8,32,1848]{2,1,0:T(8,128)(2,1)} %copy-done.16, bf16[8,32,1848]{2,1,0:T(8,128)(2,1)} %copy-done.19, bf16[16,32,512]{2,1,0:T(8,128)(2,1)} %copy-done.7, bf16[1848,512]{1,0:T(8,128)(2,1)} %base.1, f32[32,1848]{1,0:T(8,128)} %wide.1, ...), custom_call_target="tpu_custom_call" | custom-call | flops 1024 | bytes 1024 | tf_op jit(solution)/shard_map/pallas_call | solution.py:24
  168.5 2.1 %collective-permute-start.26 = (bf16[136,8,128]{2,1,0:T(8,128)(2,1)S(1)}, bf16[136,8,128]{2,1,0:T(8,128)(2,1)S(1)}, u32[]{:S(2)}, u32[]{:S(2)}) collective-permute-start(bf16[136,8,128]{2,1,0:T(8,128)(2,1)S(1)} %convert_element_type.185), channel_id=1, source_target_pairs={{0,32},{1,129},{16,48},{17,145},{32,0},{33,161},{48,16},{49,177},{... | collective-permute-start | bytes 835592 | tf_op jit(solution)/shard_map/ppermute | solution.py:44
  171.4 1.7 collective-permute-start.21
  173.0 5.4 %collective-permute-done.27 = bf16[136,8,128]{2,1,0:T(8,128)(2,1)S(1)} collective-permute-done((bf16[136,8,128]{2,1,0:T(8,128)(2,1)S(1)}, bf16[136,8,128]{2,1,0:T(8,128)(2,1)S(1)}, u32[]{:S(2)}, u32[]{:S(2)}) %collective-permute-start.27) | collective-permute-done | bytes 278560 | tf_op jit(solution)/shard_map/ppermute | solution.py:44
  180.0 2.4 %collective-permute-start.29 = (bf16[136,8,128]{2,1,0:T(8,128)(2,1)S(1)}, bf16[136,8,128]{2,1,0:T(8,128)(2,1)S(1)}, u32[]{:S(2)}, u32[]{:S(2)}) collective-permute-start(bf16[136,8,128]{2,1,0:T(8,128)(2,1)S(1)} %fusion.15), channel_id=1, source_target_pairs={{0,128},{1,33},{16,144},{17,49},{32,160},{33,1},{48,176},{49,17},{... | collective-permute-start | bytes 835592 | tf_op jit(solution)/shard_map/ppermute | solution.py:44
  182.9 2.6 %collective-permute-start.22 = (bf16[78,8,128]{2,1,0:T(8,128)(2,1)S(1)}, bf16[78,8,128]{2,1,0:T(8,128)(2,1)S(1)}, u32[]{:S(2)}, u32[]{:S(2)}) collective-permute-start(bf16[78,8,128]{2,1,0:T(8,128)(2,1)S(1)} %pad_maximum_fusion.7), channel_id=1, source_target_pairs={{0,4},{2,6},{4,0},{6,2},{8,12},{10,14},{12,8},{14,10},{1,5},{3,7},... | collective-permute-start | bytes 479240 | tf_op jit(solution)/shard_map/ppermute | solution.py:52
  186.1 3.4 %collective-permute-done.29 = bf16[136,8,128]{2,1,0:T(8,128)(2,1)S(1)} collective-permute-done((bf16[136,8,128]{2,1,0:T(8,128)(2,1)S(1)}, bf16[136,8,128]{2,1,0:T(8,128)(2,1)S(1)}, u32[]{:S(2)}, u32[]{:S(2)}) %collective-permute-start.29) | collective-permute-done | bytes 278560 | tf_op jit(solution)/shard_map/ppermute | solution.py:44
  190.6 1.6 collective-permute-done.22
  192.3 6.7 %collective-permute-start.23 = (bf16[62,8,128]{2,1,0:T(8,128)(2,1)S(1)}, bf16[62,8,128]{2,1,0:T(8,128)(2,1)S(1)}, u32[]{:S(2)}, u32[]{:S(2)}) collective-permute-start(bf16[62,8,128]{2,1,0:T(8,128)(2,1)S(1)} %pad_maximum_fusion.9), channel_id=1, source_target_pairs={{0,8},{2,10},{4,12},{6,14},{8,0},{10,2},{12,4},{14,6},{1,9},{3,11}... | collective-permute-start | bytes 380936 | tf_op jit(solution)/shard_map/ppermute | solution.py:52
  199.8 2.2 %collective-permute-done.23 = bf16[62,8,128]{2,1,0:T(8,128)(2,1)S(1)} collective-permute-done((bf16[62,8,128]{2,1,0:T(8,128)(2,1)S(1)}, bf16[62,8,128]{2,1,0:T(8,128)(2,1)S(1)}, u32[]{:S(2)}, u32[]{:S(2)}) %collective-permute-start.23) | collective-permute-done | bytes 127008 | tf_op jit(solution)/shard_map/ppermute | solution.py:52
  202.1 4.2 %collective-permute-start.24 = (f32[46,8,128]{2,1,0:T(8,128)S(1)}, f32[46,8,128]{2,1,0:T(8,128)S(1)}, u32[]{:S(2)}, u32[]{:S(2)}) collective-permute-start(f32[46,8,128]{2,1,0:T(8,128)S(1)} %slice_add_fusion.2), channel_id=1, source_target_pairs={{0,1},{1,0},{2,3},{3,2},{4,5},{5,4},{6,7},{7,6},{8,9},{9,8},{10,11... | collective-permute-start | bytes 565256 | tf_op jit(solution)/shard_map/ppermute | solution.py:56
  (117 shorter events, 22.3 us)
Async XLA Ops:
  0.6 23.0 %copy-start.14 = (f32[32,512]{1,0:T(8,128)S(1)}, f32[32,512]{1,0:T(8,128)}, u32[]{:S(2)}) copy-start(f32[32,512]{1,0:T(8,128)} %narrow.1) | copy-start | bytes 196612
  0.6 23.0 %copy-start.4 = (bf16[1848,512]{1,0:T(8,128)(2,1)S(1)}, bf16[1848,512]{1,0:T(8,128)(2,1)}, u32[]{:S(2)}) copy-start(bf16[1848,512]{1,0:T(8,128)(2,1)} %base.1) | copy-start | bytes 5677060
  0.7 16.2 %collective-permute-start = (bf16[1,32,512]{2,1,0:T(8,128)(2,1)}, bf16[1,32,512]{2,1,0:T(8,128)(2,1)S(1)}, u32[]{:S(2)}, u32[]{:S(2)}) collective-permute-start(bf16[1,32,512]{2,1,0:T(8,128)(2,1)} %bitcast.93), channel_id=1, source_target_pairs={{0,8},{2,10},{4,12},{6,14},{8,0},{10,2},{12,4},{14,6},{1,9},{3,11}... | collective-permute-start | bytes 98312 | tf_op jit(solution)/shard_map/ppermute | solution.py:52
  10.1 18.5 %all-to-all-start = ((bf16[16,32,512]{2,1,0:T(8,128)(2,1)}), bf16[16,32,512]{2,1,0:T(8,128)(2,1)S(1)}, u32[]{:S(2)}, u32[]{:S(2)}) async-start(bf16[16,32,512]{2,1,0:T(8,128)(2,1)} %broadcast_in_dim.7), calls=%async_computation | async-start | bytes 1048576 | tf_op jit(solution)/shard_map/all_to_all | solution.py:92
  17.6 5.0 %collective-permute-start.1 = (bf16[2,32,512]{2,1,0:T(8,128)(2,1)S(1)}, bf16[2,32,512]{2,1,0:T(8,128)(2,1)S(1)}, u32[]{:S(2)}, u32[]{:S(2)}) collective-permute-start(bf16[2,32,512]{2,1,0:T(8,128)(2,1)S(1)} %pad_maximum_fusion.10), channel_id=1, source_target_pairs={{0,4},{2,6},{4,0},{6,2},{8,12},{10,14},{12,8},{14,10},{1,5},{3,7},... | collective-permute-start | bytes 196616 | tf_op jit(solution)/shard_map/ppermute | solution.py:52
  23.4 4.2 %collective-permute-start.2 = (bf16[4,32,512]{2,1,0:T(8,128)(2,1)S(1)}, bf16[4,32,512]{2,1,0:T(8,128)(2,1)}, u32[]{:S(2)}, u32[]{:S(2)}) collective-permute-start(bf16[4,32,512]{2,1,0:T(8,128)(2,1)S(1)} %pad_maximum_fusion.8), channel_id=1, source_target_pairs={{0,2},{2,0},{4,6},{6,4},{8,10},{10,8},{12,14},{14,12},{1,3},{3,1},... | collective-permute-start | bytes 393224 | tf_op jit(solution)/shard_map/ppermute | solution.py:52
  24.6 15.3 %copy-start.15 = (s32[4]{0:T(128)}, s32[4]{0:T(128)S(1)}, u32[]{:S(2)}) copy-start(s32[4]{0:T(128)S(1)} %pad_add_fusion.ids) | copy-start | bytes 52
  24.6 10.6 %copy-start.8 = (f32[32,1848]{1,0:T(8,128)S(1)}, f32[32,1848]{1,0:T(8,128)}, u32[]{:S(2)}) copy-start(f32[32,1848]{1,0:T(8,128)} %refs_0_.3) | copy-start | bytes 709636
  24.6 10.6 %copy-start.9 = (f32[32,1848]{1,0:T(8,128)S(1)}, f32[32,1848]{1,0:T(8,128)}, u32[]{:S(2)}) copy-start(f32[32,1848]{1,0:T(8,128)} %refs_1_.3) | copy-start | bytes 709636
  24.6 10.6 %copy-start.12 = (f32[32,512]{1,0:T(8,128)S(1)}, f32[32,512]{1,0:T(8,128)}, u32[]{:S(2)}) copy-start(f32[32,512]{1,0:T(8,128)} %refs_2_.5) | copy-start | bytes 196612
  24.6 10.6 %copy-start.13 = (f32[32,512]{1,0:T(8,128)S(1)}, f32[32,512]{1,0:T(8,128)}, u32[]{:S(2)}) copy-start(f32[32,512]{1,0:T(8,128)} %refs_3_.3) | copy-start | bytes 196612
  27.1 8.1 %copy-start = (bf16[512,1848]{0,1:T(8,128)(2,1)S(1)}, bf16[512,1848]{0,1:T(8,128)(2,1)}, u32[]{:S(2)}) copy-start(bf16[512,1848]{0,1:T(8,128)(2,1)} %param.13) | copy-start | bytes 5677060
  30.1 8.3 %copy-start.7 = (bf16[16,32,512]{2,1,0:T(8,128)(2,1)}, bf16[16,32,512]{2,1,0:T(8,128)(2,1)S(1)}, u32[]{:S(2)}) copy-start(bf16[16,32,512]{2,1,0:T(8,128)(2,1)S(1)} %all-to-all-done.cot) | copy-start | bytes 1572868
  32.0 6.5 %collective-permute-start.4 = (bf16[8,32,1848]{2,1,0:T(8,128)(2,1)S(1)}, bf16[8,32,1848]{2,1,0:T(8,128)(2,1)S(1)}, u32[]{:S(2)}, u32[]{:S(2)}) collective-permute-start(bf16[8,32,1848]{2,1,0:T(8,128)(2,1)S(1)} %get-tuple-element.33), channel_id=1, source_target_pairs={{0,1},{1,0},{2,3},{3,2},{4,5},{5,4},{6,7},{7,6},{8,9},{9,8},{10,11... | collective-permute-start | bytes 2838536 | tf_op jit(solution)/shard_map/ppermute | solution.py:56
  35.1 4.8 %collective-permute-start.3 = (bf16[8,32,512]{2,1,0:T(8,128)(2,1)S(1)}, bf16[8,32,512]{2,1,0:T(8,128)(2,1)S(1)}, u32[]{:S(2)}, u32[]{:S(2)}) collective-permute-start(bf16[8,32,512]{2,1,0:T(8,128)(2,1)S(1)} %pad_maximum_fusion.2.act_own), channel_id=1, source_target_pairs={{0,1},{1,0},{2,3},{3,2},{4,5},{5,4},{6,7},{7,6},{8,9},{9,8},{10,11... | collective-permute-start | bytes 786440 | tf_op jit(solution)/shard_map/ppermute | solution.py:56
  38.4 5.6 %copy-start.2 = (bf16[1848,512]{1,0:T(8,128)(2,1)}, bf16[1848,512]{1,0:T(8,128)(2,1)S(1)}, u32[]{:S(2)}) copy-start(bf16[1848,512]{1,0:T(8,128)(2,1)S(1)} %get-tuple-element.29.gate_eff) | copy-start | bytes 5677060
  38.5 5.6 %copy-start.3 = (bf16[1848,512]{1,0:T(8,128)(2,1)}, bf16[1848,512]{1,0:T(8,128)(2,1)S(1)}, u32[]{:S(2)}) copy-start(bf16[1848,512]{1,0:T(8,128)(2,1)S(1)} %get-tuple-element.30.up_eff) | copy-start | bytes 5677060
  44.8 15.0 %collective-permute-start.6 = (bf16[4,2,32,1848]{3,2,1,0:T(8,128)(2,1)}, bf16[4,2,32,1848]{3,2,1,0:T(8,128)(2,1)}, u32[]{:S(2)}, u32[]{:S(2)}) collective-permute-start(bf16[4,2,32,1848]{3,2,1,0:T(8,128)(2,1)} %get-tuple-element.38), channel_id=1, source_target_pairs={{0,16},{1,65},{16,32},{17,81},{32,48},{33,97},{48,0},{49,113},{64,... | collective-permute-start | bytes 2838536 | tf_op jit(solution)/shard_map/ppermute | solution.py:44
  46.5 25.0 %collective-permute-start.7 = (bf16[4,2,32,1848]{3,2,1,0:T(8,128)(2,1)}, bf16[4,2,32,1848]{3,2,1,0:T(8,128)(2,1)}, u32[]{:S(2)}, u32[]{:S(2)}) collective-permute-start(bf16[4,2,32,1848]{3,2,1,0:T(8,128)(2,1)} %get-tuple-element.39), channel_id=1, source_target_pairs={{0,32},{1,129},{16,48},{17,145},{32,0},{33,161},{48,16},{49,177},{... | collective-permute-start | bytes 2838536 | tf_op jit(solution)/shard_map/ppermute | solution.py:44
  48.9 22.6 %collective-permute-start.8 = (bf16[4,2,32,1848]{3,2,1,0:T(8,128)(2,1)S(1)}, bf16[4,2,32,1848]{3,2,1,0:T(8,128)(2,1)}, u32[]{:S(2)}, u32[]{:S(2)}) collective-permute-start(bf16[4,2,32,1848]{3,2,1,0:T(8,128)(2,1)S(1)} %get-tuple-element.40), channel_id=1, source_target_pairs={{0,48},{1,193},{16,0},{17,209},{32,16},{33,225},{48,32},{49,241},{... | collective-permute-start | bytes 2838536 | tf_op jit(solution)/shard_map/ppermute | solution.py:44
  50.1 31.3 %all-to-all-start.1 = ((bf16[8,32,1848]{2,1,0:T(8,128)(2,1)}), bf16[8,32,1848]{2,1,0:T(8,128)(2,1)S(1)}, u32[]{:S(2)}, u32[]{:S(2)}) async-start(bf16[8,32,1848]{2,1,0:T(8,128)(2,1)} %add_convert_fusion), calls=%async_computation.1 | async-start | bytes 1966080 | tf_op jit(solution)/shard_map/all_to_all | solution.py:92
  73.6 11.6 %collective-permute-start.9 = (bf16[2,32,1848]{2,1,0:T(8,128)(2,1)S(1)}, bf16[2,32,1848]{2,1,0:T(8,128)(2,1)S(1)}, u32[]{:S(2)}, u32[]{:S(2)}) collective-permute-start(bf16[2,32,1848]{2,1,0:T(8,128)(2,1)S(1)} %get-tuple-element.51), channel_id=1, source_target_pairs={{0,64},{1,17},{16,80},{17,33},{32,96},{33,49},{48,112},{49,1},{64,... | collective-permute-start | bytes 709640 | tf_op jit(solution)/shard_map/ppermute | solution.py:44
  74.7 10.5 %collective-permute-start.11 = (bf16[2,32,1848]{2,1,0:T(8,128)(2,1)S(1)}, bf16[2,32,1848]{2,1,0:T(8,128)(2,1)S(1)}, u32[]{:S(2)}, u32[]{:S(2)}) collective-permute-start(bf16[2,32,1848]{2,1,0:T(8,128)(2,1)S(1)} %get-tuple-element.52), channel_id=1, source_target_pairs={{0,192},{1,49},{16,208},{17,1},{32,224},{33,17},{48,240},{49,33},{... | collective-permute-start | bytes 709640 | tf_op jit(solution)/shard_map/ppermute | solution.py:44
  76.3 8.9 %collective-permute-start.10 = (bf16[2,32,1848]{2,1,0:T(8,128)(2,1)S(1)}, bf16[2,32,1848]{2,1,0:T(8,128)(2,1)S(1)}, u32[]{:S(2)}, u32[]{:S(2)}) collective-permute-start(bf16[2,32,1848]{2,1,0:T(8,128)(2,1)S(1)} %get-tuple-element.53), channel_id=1, source_target_pairs={{0,128},{1,33},{16,144},{17,49},{32,160},{33,1},{48,176},{49,17},{... | collective-permute-start | bytes 709640 | tf_op jit(solution)/shard_map/ppermute | solution.py:44
  82.1 12.6 %collective-permute-start.5 = (bf16[32,1848]{1,0:T(8,128)(2,1)}, bf16[32,1848]{1,0:T(8,128)(2,1)S(1)}, u32[]{:S(2)}, u32[]{:S(2)}) collective-permute-start(bf16[32,1848]{1,0:T(8,128)(2,1)} %reduce_sum.12), channel_id=1, source_target_pairs={{0,224},{1,160},{2,128},{3,144},{4,80},{5,240},{6,48},{7,64},{8,0}... | collective-permute-start | bytes 354824 | tf_op jit(solution)/shard_map/ppermute | solution.py:76
  95.0 7.0 %collective-permute-start.13 = (bf16[2,32,1848]{2,1,0:T(8,128)(2,1)S(1)}, bf16[2,32,1848]{2,1,0:T(8,128)(2,1)S(1)}, u32[]{:S(2)}, u32[]{:S(2)}) collective-permute-start(bf16[2,32,1848]{2,1,0:T(8,128)(2,1)S(1)} %get-tuple-element.64), channel_id=1, source_target_pairs={{0,128},{1,33},{16,144},{17,49},{32,160},{33,1},{48,176},{49,17},{... | collective-permute-start | bytes 709640 | tf_op jit(solution)/shard_map/ppermute | solution.py:44
  95.1 8.6 %collective-permute-start.12 = (bf16[2,32,1848]{2,1,0:T(8,128)(2,1)S(1)}, bf16[2,32,1848]{2,1,0:T(8,128)(2,1)S(1)}, u32[]{:S(2)}, u32[]{:S(2)}) collective-permute-start(bf16[2,32,1848]{2,1,0:T(8,128)(2,1)S(1)} %get-tuple-element.64), channel_id=1, source_target_pairs={{0,192},{1,49},{16,208},{17,1},{32,224},{33,17},{48,240},{49,33},{... | collective-permute-start | bytes 709640 | tf_op jit(solution)/shard_map/ppermute | solution.py:44
  96.2 8.4 %collective-permute-start.14 = (bf16[2,32,1848]{2,1,0:T(8,128)(2,1)S(1)}, bf16[2,32,1848]{2,1,0:T(8,128)(2,1)S(1)}, u32[]{:S(2)}, u32[]{:S(2)}) collective-permute-start(bf16[2,32,1848]{2,1,0:T(8,128)(2,1)S(1)} %get-tuple-element.64), channel_id=1, source_target_pairs={{0,64},{1,17},{16,80},{17,33},{32,96},{33,49},{48,112},{49,1},{64,... | collective-permute-start | bytes 709640 | tf_op jit(solution)/shard_map/ppermute | solution.py:44
  96.6 14.7 %collective-permute-start.15 = (bf16[32,1848]{1,0:T(8,128)(2,1)S(1)}, bf16[32,1848]{1,0:T(8,128)(2,1)S(1)}, u32[]{:S(2)}, u32[]{:S(2)}) collective-permute-start(bf16[32,1848]{1,0:T(8,128)(2,1)S(1)} %get-tuple-element.60), channel_id=1, source_target_pairs={{224,0},{160,1},{128,2},{144,3},{80,4},{240,5},{48,6},{64,7},{0,8}... | collective-permute-start | bytes 354824 | tf_op jit(solution)/shard_map/ppermute | solution.py:80
  104.7 39.8 %copy-start.17 = (bf16[4,2,32,1848]{3,2,1,0:T(8,128)(2,1)}, bf16[4,2,32,1848]{3,2,1,0:T(8,128)(2,1)S(1)}, u32[]{:S(2)}) copy-start(bf16[4,2,32,1848]{3,2,1,0:T(8,128)(2,1)S(1)} %pad_maximum_fusion.g0) | copy-start | bytes 2838532
  112.4 31.6 %all-to-all-start.2 = ((bf16[8,32,1848]{2,1,0:T(8,128)(2,1)}), bf16[8,32,1848]{2,1,0:T(8,128)(2,1)S(1)}, u32[]{:S(2)}, u32[]{:S(2)}) async-start(bf16[8,32,1848]{2,1,0:T(8,128)(2,1)} %broadcast_in_dim.8), calls=%async_computation.2 | async-start | bytes 1966080 | tf_op jit(solution)/shard_map/all_to_all | solution.py:92
  116.2 28.3 %collective-permute-start.18 = (bf16[4,2,32,1848]{3,2,1,0:T(8,128)(2,1)S(1)}, bf16[4,2,32,1848]{3,2,1,0:T(8,128)(2,1)}, u32[]{:S(2)}, u32[]{:S(2)}) collective-permute-start(bf16[4,2,32,1848]{3,2,1,0:T(8,128)(2,1)S(1)} %pad_maximum_fusion.g0), channel_id=1, source_target_pairs={{0,16},{1,65},{16,32},{17,81},{32,48},{33,97},{48,0},{49,113},{64,... | collective-permute-start | bytes 2838536 | tf_op jit(solution)/shard_map/ppermute | solution.py:44
  116.3 28.1 %collective-permute-start.17 = (bf16[4,2,32,1848]{3,2,1,0:T(8,128)(2,1)S(1)}, bf16[4,2,32,1848]{3,2,1,0:T(8,128)(2,1)}, u32[]{:S(2)}, u32[]{:S(2)}) collective-permute-start(bf16[4,2,32,1848]{3,2,1,0:T(8,128)(2,1)S(1)} %pad_maximum_fusion.g0), channel_id=1, source_target_pairs={{0,32},{1,129},{16,48},{17,145},{32,0},{33,161},{48,16},{49,177},{... | collective-permute-start | bytes 2838536 | tf_op jit(solution)/shard_map/ppermute | solution.py:44
  117.4 27.1 %collective-permute-start.16 = (bf16[4,2,32,1848]{3,2,1,0:T(8,128)(2,1)S(1)}, bf16[4,2,32,1848]{3,2,1,0:T(8,128)(2,1)}, u32[]{:S(2)}, u32[]{:S(2)}) collective-permute-start(bf16[4,2,32,1848]{3,2,1,0:T(8,128)(2,1)S(1)} %pad_maximum_fusion.g0), channel_id=1, source_target_pairs={{0,48},{1,193},{16,0},{17,209},{32,16},{33,225},{48,32},{49,241},{... | collective-permute-start | bytes 2838536 | tf_op jit(solution)/shard_map/ppermute | solution.py:44
  144.0 14.1 %copy-start.16 = (bf16[8,32,1848]{2,1,0:T(8,128)(2,1)}, bf16[8,32,1848]{2,1,0:T(8,128)(2,1)S(1)}, u32[]{:S(2)}) copy-start(bf16[8,32,1848]{2,1,0:T(8,128)(2,1)S(1)} %all-to-all-done.2.hid_own) | copy-start | bytes 2838532
  144.0 15.4 %collective-permute-start.19 = (bf16[8,32,1848]{2,1,0:T(8,128)(2,1)S(1)}, bf16[8,32,1848]{2,1,0:T(8,128)(2,1)S(1)}, u32[]{:S(2)}, u32[]{:S(2)}) collective-permute-start(bf16[8,32,1848]{2,1,0:T(8,128)(2,1)S(1)} %all-to-all-done.2.hid_own), channel_id=1, source_target_pairs={{0,1},{1,0},{2,3},{3,2},{4,5},{5,4},{6,7},{7,6},{8,9},{9,8},{10,11... | collective-permute-start | bytes 2838536 | tf_op jit(solution)/shard_map/ppermute | solution.py:56
  159.4 7.0 %copy-start.20 = (f32[32,8,128]{2,1,0:T(8,128)S(1)}, f32[32,8,128]{2,1,0:T(8,128)}, u32[]{:S(2)}) copy-start(f32[32,8,128]{2,1,0:T(8,128)} %get-tuple-element.46) | copy-start | bytes 393220
  167.4 3.8 %collective-permute-start.20 = (f32[174,8,128]{2,1,0:T(8,128)S(1)}, f32[174,8,128]{2,1,0:T(8,128)S(1)}, u32[]{:S(2)}, u32[]{:S(2)}) collective-permute-start(f32[174,8,128]{2,1,0:T(8,128)S(1)} %pad_maximum_fusion.1), channel_id=1, source_target_pairs={{0,1},{1,0},{2,3},{3,2},{4,5},{5,4},{6,7},{7,6},{8,9},{9,8},{10,11... | collective-permute-start | bytes 2138120 | tf_op jit(solution)/shard_map/ppermute | solution.py:56
  168.4 10.0 %collective-permute-start.27 = (bf16[136,8,128]{2,1,0:T(8,128)(2,1)S(1)}, bf16[136,8,128]{2,1,0:T(8,128)(2,1)S(1)}, u32[]{:S(2)}, u32[]{:S(2)}) collective-permute-start(bf16[136,8,128]{2,1,0:T(8,128)(2,1)S(1)} %convert_element_type.185), channel_id=1, source_target_pairs={{0,16},{1,65},{16,32},{17,81},{32,48},{33,97},{48,0},{49,113},{64,... | collective-permute-start | bytes 835592 | tf_op jit(solution)/shard_map/ppermute | solution.py:44
  168.5 9.9 %collective-permute-start.26 = (bf16[136,8,128]{2,1,0:T(8,128)(2,1)S(1)}, bf16[136,8,128]{2,1,0:T(8,128)(2,1)S(1)}, u32[]{:S(2)}, u32[]{:S(2)}) collective-permute-start(bf16[136,8,128]{2,1,0:T(8,128)(2,1)S(1)} %convert_element_type.185), channel_id=1, source_target_pairs={{0,32},{1,129},{16,48},{17,145},{32,0},{33,161},{48,16},{49,177},{... | collective-permute-start | bytes 835592 | tf_op jit(solution)/shard_map/ppermute | solution.py:44
  170.6 8.4 %collective-permute-start.25 = (bf16[136,8,128]{2,1,0:T(8,128)(2,1)S(1)}, bf16[136,8,128]{2,1,0:T(8,128)(2,1)S(1)}, u32[]{:S(2)}, u32[]{:S(2)}) collective-permute-start(bf16[136,8,128]{2,1,0:T(8,128)(2,1)S(1)} %convert_element_type.185), channel_id=1, source_target_pairs={{0,48},{1,193},{16,0},{17,209},{32,16},{33,225},{48,32},{49,241},{... | collective-permute-start | bytes 835592 | tf_op jit(solution)/shard_map/ppermute | solution.py:44
  171.4 11.4 %collective-permute-start.21 = (bf16[110,8,128]{2,1,0:T(8,128)(2,1)S(1)}, bf16[110,8,128]{2,1,0:T(8,128)(2,1)S(1)}, u32[]{:S(2)}, u32[]{:S(2)}) collective-permute-start(bf16[110,8,128]{2,1,0:T(8,128)(2,1)S(1)} %pad_maximum_fusion.5), channel_id=1, source_target_pairs={{0,2},{2,0},{4,6},{6,4},{8,10},{10,8},{12,14},{14,12},{1,3},{3,1},... | collective-permute-start | bytes 675848 | tf_op jit(solution)/shard_map/ppermute | solution.py:52
  179.2 7.0 %collective-permute-start.30 = (bf16[136,8,128]{2,1,0:T(8,128)(2,1)S(1)}, bf16[136,8,128]{2,1,0:T(8,128)(2,1)S(1)}, u32[]{:S(2)}, u32[]{:S(2)}) collective-permute-start(bf16[136,8,128]{2,1,0:T(8,128)(2,1)S(1)} %fusion.15), channel_id=1, source_target_pairs={{0,64},{1,17},{16,80},{17,33},{32,96},{33,49},{48,112},{49,1},{64,... | collective-permute-start | bytes 835592 | tf_op jit(solution)/shard_map/ppermute | solution.py:44
  180.0 9.6 %collective-permute-start.29 = (bf16[136,8,128]{2,1,0:T(8,128)(2,1)S(1)}, bf16[136,8,128]{2,1,0:T(8,128)(2,1)S(1)}, u32[]{:S(2)}, u32[]{:S(2)}) collective-permute-start(bf16[136,8,128]{2,1,0:T(8,128)(2,1)S(1)} %fusion.15), channel_id=1, source_target_pairs={{0,128},{1,33},{16,144},{17,49},{32,160},{33,1},{48,176},{49,17},{... | collective-permute-start | bytes 835592 | tf_op jit(solution)/shard_map/ppermute | solution.py:44
  182.3 7.4 %collective-permute-start.28 = (bf16[136,8,128]{2,1,0:T(8,128)(2,1)S(1)}, bf16[136,8,128]{2,1,0:T(8,128)(2,1)S(1)}, u32[]{:S(2)}, u32[]{:S(2)}) collective-permute-start(bf16[136,8,128]{2,1,0:T(8,128)(2,1)S(1)} %fusion.15), channel_id=1, source_target_pairs={{0,192},{1,49},{16,208},{17,1},{32,224},{33,17},{48,240},{49,33},{... | collective-permute-start | bytes 835592 | tf_op jit(solution)/shard_map/ppermute | solution.py:44
  182.9 9.3 %collective-permute-start.22 = (bf16[78,8,128]{2,1,0:T(8,128)(2,1)S(1)}, bf16[78,8,128]{2,1,0:T(8,128)(2,1)S(1)}, u32[]{:S(2)}, u32[]{:S(2)}) collective-permute-start(bf16[78,8,128]{2,1,0:T(8,128)(2,1)S(1)} %pad_maximum_fusion.7), channel_id=1, source_target_pairs={{0,4},{2,6},{4,0},{6,2},{8,12},{10,14},{12,8},{14,10},{1,5},{3,7},... | collective-permute-start | bytes 479240 | tf_op jit(solution)/shard_map/ppermute | solution.py:52
  192.3 9.7 %collective-permute-start.23 = (bf16[62,8,128]{2,1,0:T(8,128)(2,1)S(1)}, bf16[62,8,128]{2,1,0:T(8,128)(2,1)S(1)}, u32[]{:S(2)}, u32[]{:S(2)}) collective-permute-start(bf16[62,8,128]{2,1,0:T(8,128)(2,1)S(1)} %pad_maximum_fusion.9), channel_id=1, source_target_pairs={{0,8},{2,10},{4,12},{6,14},{8,0},{10,2},{12,4},{14,6},{1,9},{3,11}... | collective-permute-start | bytes 380936 | tf_op jit(solution)/shard_map/ppermute | solution.py:52
  202.1 5.2 %collective-permute-start.24 = (f32[46,8,128]{2,1,0:T(8,128)S(1)}, f32[46,8,128]{2,1,0:T(8,128)S(1)}, u32[]{:S(2)}, u32[]{:S(2)}) collective-permute-start(f32[46,8,128]{2,1,0:T(8,128)S(1)} %slice_add_fusion.2), channel_id=1, source_target_pairs={{0,1},{1,0},{2,3},{3,2},{4,5},{5,4},{6,7},{7,6},{8,9},{9,8},{10,11... | collective-permute-start | bytes 565256 | tf_op jit(solution)/shard_map/ppermute | solution.py:56
  (10 other events, 17.1 us)

commit v2 on v1

--- a/solution.py
+++ b/solution.py
@@ -46,6 +46,10 @@
 
 def plane_shift(v, step, primary):
     return plane_permute(v, lambda i: (i + step) % 4, primary)
+
+
+def plane_swap(v, mask, primary):
+    return plane_permute(v, lambda i: i ^ mask, primary)
 
 
 def z_swap(v, mask):
@@ -358,7 +362,8 @@
 
     r_all = jnp.concatenate([r_up, r_down], axis=0)
     for primary in (True, False):
-        r_all = r_all + add_all(*gather4(r_all.astype(BF16), primary)[1:])
+        for mask in (1, 2):
+            r_all = r_all + plane_swap(r_all.astype(BF16), mask, primary).astype(F32)
 
     first = lax.axis_index("core") == 0
     l_all = jnp.concatenate([l_up, l_down], axis=0)

time: 210 us -> 209 us (level)
  starting transfers between devices: 71.1 us -> 67.7 us
  waiting for transfers between devices: 83.2 us -> 85.9 us
    ppermute x18 -> x16, starting transfers between devices: 20.3 us -> 17 us  [plane_permute(): return lax.ppermute(v, ('y', 'x', 'core'), perm)]
    ppermute x18 -> x16, waiting for transfers between devices: 31.4 us -> 34.1 us  [plane_permute(): return lax.ppermute(v, ('y', 'x', 'core'), perm)]
  transfers between devices with their start and end apart: 34 -> 32, of which waited for: 19 -> 17; matrix products, arithmetic and copies ran while one was open for 7% -> 7% of each run, Pallas kernels for 8% -> 8%
where the time goes in v2:
time: 209 us; the launch traced here: 208 us
  waiting for transfers between devices  85.9 us (41%)
  starting transfers between devices  67.7 us (32%)
  Pallas kernels  28.4 us (14%)
  local copies, waits for them, and re-layouts  13.2 us (6%)
  other arithmetic  11.9 us (6%)
    ppermute x16, waiting for transfers between devices, plane_permute(): return lax.ppermute(v, ('y', 'x', 'core'), perm)  34.1 us
    pallas_call x6, Pallas kernels, kernel_call(): pl.pallas_call(body, out_shape=[jax.ShapeDtypeStruct(s, d) for s, d in ou...  28.4 us
    all_to_all x3, waiting for transfers between devices, to_all(): return lax.all_to_all(v, axis, split_axis=0, concat_axis=0, tiled=True)  28.4 us
    ppermute x6, starting transfers between devices, z_swap(): return lax.ppermute(v, 'z', [(i, i ^ mask) for i in range(NZ)])  20.1 us
    ppermute x16, starting transfers between devices, plane_permute(): return lax.ppermute(v, ('y', 'x', 'core'), perm)  17 us
    all_to_all x3, starting transfers between devices, to_all(): return lax.all_to_all(v, axis, split_axis=0, concat_axis=0, tiled=True)  14.1 us
    ppermute x5, starting transfers between devices, core_swap(): return lax.ppermute(v, 'core', [(0, 1), (1, 0)])  8.8 us
    ppermute x1, waiting for transfers between devices, to_columns(): return lax.ppermute(v, ('y', 'x', 'z', 'core'), grid_pairs())  8.3 us
  transfers between devices with their start and end apart: 32, of which 17 were waited for; matrix products, arithmetic and copies ran while one was open for 7% of the time, Pallas kernels for 8%

profile of v2, /device:TPU:1, one launch (start us, length us, event | category | flops | bytes accessed | tf_op | source)
XLA Modules:
  0.0 208.3 jit_solution(17856820393641055789)
XLA Ops:
  0.7 7.8 %collective-permute-start = (bf16[1,32,512]{2,1,0:T(8,128)(2,1)}, bf16[1,32,512]{2,1,0:T(8,128)(2,1)S(1)}, u32[]{:S(2)}, u32[]{:S(2)}) collective-permute-start(bf16[1,32,512]{2,1,0:T(8,128)(2,1)} %bitcast.93), channel_id=1, source_target_pairs={{0,8},{2,10},{4,12},{6,14},{8,0},{10,2},{12,4},{14,6},{1,9},{3,11}... | collective-permute-start | bytes 98312 | tf_op jit(solution)/shard_map/ppermute | solution.py:56
  8.5 1.6 broadcast_in_dim.7
  10.1 6.8 %all-to-all-start = ((bf16[16,32,512]{2,1,0:T(8,128)(2,1)}), bf16[16,32,512]{2,1,0:T(8,128)(2,1)S(1)}, u32[]{:S(2)}, u32[]{:S(2)}) async-start(bf16[16,32,512]{2,1,0:T(8,128)(2,1)} %broadcast_in_dim.7), calls=%async_computation | async-start | bytes 1048576 | tf_op jit(solution)/shard_map/all_to_all | solution.py:96
  17.6 1.2 collective-permute-start.1
  18.8 3.8 %collective-permute-done.1 = bf16[2,32,512]{2,1,0:T(8,128)(2,1)S(1)} collective-permute-done((bf16[2,32,512]{2,1,0:T(8,128)(2,1)S(1)}, bf16[2,32,512]{2,1,0:T(8,128)(2,1)S(1)}, u32[]{:S(2)}, u32[]{:S(2)}) %collective-permute-start.1) | collective-permute-done | bytes 65568 | tf_op jit(solution)/shard_map/ppermute | solution.py:56
  24.6 1.2 shard_map.163.eff
  25.8 1.3 copy-done.5
  28.6 1.5 copy-done.6
  30.1 1.8 shard_map.164
  32.0 3.1 %collective-permute-start.4 = (bf16[8,32,1848]{2,1,0:T(8,128)(2,1)S(1)}, bf16[8,32,1848]{2,1,0:T(8,128)(2,1)S(1)}, u32[]{:S(2)}, u32[]{:S(2)}) collective-permute-start(bf16[8,32,1848]{2,1,0:T(8,128)(2,1)S(1)} %get-tuple-element.33), channel_id=1, source_target_pairs={{0,1},{1,0},{2,3},{3,2},{4,5},{5,4},{6,7},{7,6},{8,9},{9,8},{10,11... | collective-permute-start | bytes 2838536 | tf_op jit(solution)/shard_map/ppermute | solution.py:60
  35.2 1.5 copy-done.1
  36.7 1.7 shard_map.162
  38.5 1.4 add_convert_fusion
  39.9 4.2 %shard_map.165 = (bf16[4,2,32,1848]{3,2,1,0:T(8,128)(2,1)S(1)}, bf16[4,2,32,1848]{3,2,1,0:T(8,128)(2,1)}, bf16[4,2,32,1848]{3,2,1,0:T(8,128)(2,1)}, bf16[4,2,32,...) custom-call(s32[4]{0:T(128)S(1)} %pad_add_fusion.ids, bf16[8,32,512]{2,1,0:T(8,128)(2,1)S(1)} %pad_maximum_fusion.2.act_own, ...), custom_call_target="tpu_custom_call" | custom-call | flops 1024 | bytes 1024 | tf_op jit(solution)/shard_map/pallas_call | solution.py:24
  44.9 1.6 collective-permute-start.6
  46.5 2.4 %collective-permute-start.7 = (bf16[4,2,32,1848]{3,2,1,0:T(8,128)(2,1)}, bf16[4,2,32,1848]{3,2,1,0:T(8,128)(2,1)}, u32[]{:S(2)}, u32[]{:S(2)}) collective-permute-start(bf16[4,2,32,1848]{3,2,1,0:T(8,128)(2,1)} %get-tuple-element.39), channel_id=1, source_target_pairs={{0,32},{1,129},{16,48},{17,145},{32,0},{33,161},{48,16},{49,177},{... | collective-permute-start | bytes 2838536 | tf_op jit(solution)/shard_map/ppermute | solution.py:44
  48.9 1.2 collective-permute-start.8
  50.1 3.6 %all-to-all-start.1 = ((bf16[8,32,1848]{2,1,0:T(8,128)(2,1)}), bf16[8,32,1848]{2,1,0:T(8,128)(2,1)S(1)}, u32[]{:S(2)}, u32[]{:S(2)}) async-start(bf16[8,32,1848]{2,1,0:T(8,128)(2,1)} %add_convert_fusion), calls=%async_computation.1 | async-start | bytes 1966080 | tf_op jit(solution)/shard_map/all_to_all | solution.py:96
  53.7 6.2 %collective-permute-done.6 = bf16[4,2,32,1848]{3,2,1,0:T(8,128)(2,1)} collective-permute-done((bf16[4,2,32,1848]{3,2,1,0:T(8,128)(2,1)}, bf16[4,2,32,1848]{3,2,1,0:T(8,128)(2,1)}, u32[]{:S(2)}, u32[]{:S(2)}) %collective-permute-start.6) | collective-permute-done | bytes 946208 | tf_op jit(solution)/shard_map/ppermute | solution.py:44
  59.8 11.7 %collective-permute-done.7 = bf16[4,2,32,1848]{3,2,1,0:T(8,128)(2,1)} collective-permute-done((bf16[4,2,32,1848]{3,2,1,0:T(8,128)(2,1)}, bf16[4,2,32,1848]{3,2,1,0:T(8,128)(2,1)}, u32[]{:S(2)}, u32[]{:S(2)}) %collective-permute-start.7) | collective-permute-done | bytes 946208 | tf_op jit(solution)/shard_map/ppermute | solution.py:44
  71.5 2.0 fusion.9
  73.6 1.2 collective-permute-start.9
  74.7 1.6 collective-permute-start.11
  76.3 1.2 collective-permute-start.10
  77.5 3.8 %all-to-all-done.1 = bf16[8,32,1848]{2,1,0:T(8,128)(2,1)S(1)} async-done(((bf16[8,32,1848]{2,1,0:T(8,128)(2,1)}), bf16[8,32,1848]{2,1,0:T(8,128)(2,1)S(1)}, u32[]{:S(2)}, u32[]{:S(2)}) %all-to-all-start.1) | async-done | bytes 946208 | tf_op jit(solution)/shard_map/all_to_all | solution.py:96
  82.1 3.1 %collective-permute-start.5 = (bf16[32,1848]{1,0:T(8,128)(2,1)}, bf16[32,1848]{1,0:T(8,128)(2,1)S(1)}, u32[]{:S(2)}, u32[]{:S(2)}) collective-permute-start(bf16[32,1848]{1,0:T(8,128)(2,1)} %reduce_sum.12), channel_id=1, source_target_pairs={{0,224},{1,160},{2,128},{3,144},{4,80},{5,240},{6,48},{7,64},{8,0}... | collective-permute-start | bytes 354824 | tf_op jit(solution)/shard_map/ppermute | solution.py:80
  85.2 1.4 fusion.1
  86.6 8.3 %collective-permute-done.5 = bf16[32,1848]{1,0:T(8,128)(2,1)S(1)} collective-permute-done((bf16[32,1848]{1,0:T(8,128)(2,1)}, bf16[32,1848]{1,0:T(8,128)(2,1)S(1)}, u32[]{:S(2)}, u32[]{:S(2)}) %collective-permute-start.5) | collective-permute-done | bytes 118304 | tf_op jit(solution)/shard_map/ppermute | solution.py:80
  96.8 4.6 %collective-permute-start.15 = (bf16[32,1848]{1,0:T(8,128)(2,1)S(1)}, bf16[32,1848]{1,0:T(8,128)(2,1)S(1)}, u32[]{:S(2)}, u32[]{:S(2)}) collective-permute-start(bf16[32,1848]{1,0:T(8,128)(2,1)S(1)} %get-tuple-element.60), channel_id=1, source_target_pairs={{224,0},{160,1},{128,2},{144,3},{80,4},{240,5},{48,6},{64,7},{0,8}... | collective-permute-start | bytes 354824 | tf_op jit(solution)/shard_map/ppermute | solution.py:84
  102.1 1.5 collective-permute-done.12
  104.9 6.5 %collective-permute-done.15 = bf16[32,1848]{1,0:T(8,128)(2,1)S(1)} collective-permute-done((bf16[32,1848]{1,0:T(8,128)(2,1)S(1)}, bf16[32,1848]{1,0:T(8,128)(2,1)S(1)}, u32[]{:S(2)}, u32[]{:S(2)}) %collective-permute-start.15) | collective-permute-done | bytes 118304 | tf_op jit(solution)/shard_map/ppermute | solution.py:84
  112.4 3.8 %all-to-all-start.2 = ((bf16[8,32,1848]{2,1,0:T(8,128)(2,1)}), bf16[8,32,1848]{2,1,0:T(8,128)(2,1)S(1)}, u32[]{:S(2)}, u32[]{:S(2)}) async-start(bf16[8,32,1848]{2,1,0:T(8,128)(2,1)} %broadcast_in_dim.8), calls=%async_computation.2 | async-start | bytes 1966080 | tf_op jit(solution)/shard_map/all_to_all | solution.py:96
  116.2 1.2 collective-permute-start.17
  117.4 2.0 collective-permute-start.16
  119.4 24.6 %all-to-all-done.2.hid_own = bf16[8,32,1848]{2,1,0:T(8,128)(2,1)S(1)} async-done(((bf16[8,32,1848]{2,1,0:T(8,128)(2,1)}), bf16[8,32,1848]{2,1,0:T(8,128)(2,1)S(1)}, u32[]{:S(2)}, u32[]{:S(2)}) %all-to-all-start.2) | async-done | bytes 946208 | tf_op jit(solution)/shard_map/all_to_all | solution.py:96
  144.5 13.6 %shard_map.166 = (f32[2,8,16,8,128]{4,3,2,1,0:T(8,128)}, f32[32,8,128]{2,1,0:T(8,128)}, f32[120,8,128]{2,1,0:T(8,128)}) custom-call(s32[4]{0:T(128)} %copy-done.15, bf16[1848,512]{1,0:T(8,128)(2,1)} %bitcast.88, bf16[1848,512]{1,0:T(8,128)(2,1)} %copy-done.2, bf16[1848,512]{1,0:T(8,128)(2,1)} %bitcast.90, bf16[1848,512]{1,0:T(8,128)(2,1)} %copy-done.3, ...), custom_call_target="tpu_custom_call" | custom-call | flops 1024 | bytes 1024 | tf_op jit(solution)/shard_map/pallas_call | solution.py:24
  158.1 1.3 fusion.21
  160.4 5.9 %shard_map.167 = (f32[60,8,128]{2,1,0:T(8,128)}, f32[16,8,128]{2,1,0:T(8,128)}) custom-call(s32[4]{0:T(128)} %copy-done.15, bf16[8,32,1848]{2,1,0:T(8,128)(2,1)} %copy-done.16, bf16[8,32,1848]{2,1,0:T(8,128)(2,1)} %copy-done.19, bf16[16,32,512]{2,1,0:T(8,128)(2,1)} %copy-done.7, bf16[1848,512]{1,0:T(8,128)(2,1)} %base.1, f32[32,1848]{1,0:T(8,128)} %wide.1, ...), custom_call_target="tpu_custom_call" | custom-call | flops 1024 | bytes 1024 | tf_op jit(solution)/shard_map/pallas_call | solution.py:24
  168.6 5.7 %collective-permute-done.25 = bf16[136,8,128]{2,1,0:T(8,128)(2,1)S(1)} collective-permute-done((bf16[136,8,128]{2,1,0:T(8,128)(2,1)S(1)}, bf16[136,8,128]{2,1,0:T(8,128)(2,1)S(1)}, u32[]{:S(2)}, u32[]{:S(2)}) %collective-permute-start.25) | collective-permute-done | bytes 278560 | tf_op jit(solution)/shard_map/ppermute | solution.py:44
  175.3 1.7 collective-permute-start.21
  177.0 4.6 %collective-permute-done.26 = bf16[136,8,128]{2,1,0:T(8,128)(2,1)S(1)} collective-permute-done((bf16[136,8,128]{2,1,0:T(8,128)(2,1)S(1)}, bf16[136,8,128]{2,1,0:T(8,128)(2,1)S(1)}, u32[]{:S(2)}, u32[]{:S(2)}) %collective-permute-start.26) | collective-permute-done | bytes 278560 | tf_op jit(solution)/shard_map/ppermute | solution.py:44
  182.4 2.6 %collective-permute-start.22 = (bf16[78,8,128]{2,1,0:T(8,128)(2,1)S(1)}, bf16[78,8,128]{2,1,0:T(8,128)(2,1)S(1)}, u32[]{:S(2)}, u32[]{:S(2)}) collective-permute-start(bf16[78,8,128]{2,1,0:T(8,128)(2,1)S(1)} %pad_maximum_fusion.7), channel_id=1, source_target_pairs={{0,4},{2,6},{4,0},{6,2},{8,12},{10,14},{12,8},{14,10},{1,5},{3,7},... | collective-permute-start | bytes 479240 | tf_op jit(solution)/shard_map/ppermute | solution.py:56
  184.9 2.6 %collective-permute-done.27 = bf16[136,8,128]{2,1,0:T(8,128)(2,1)S(1)} collective-permute-done((bf16[136,8,128]{2,1,0:T(8,128)(2,1)S(1)}, bf16[136,8,128]{2,1,0:T(8,128)(2,1)S(1)}, u32[]{:S(2)}, u32[]{:S(2)}) %collective-permute-start.27) | collective-permute-done | bytes 278560 | tf_op jit(solution)/shard_map/ppermute | solution.py:44
  187.6 1.7 collective-permute-start.28
  189.3 2.4 %collective-permute-done.22 = bf16[78,8,128]{2,1,0:T(8,128)(2,1)S(1)} collective-permute-done((bf16[78,8,128]{2,1,0:T(8,128)(2,1)S(1)}, bf16[78,8,128]{2,1,0:T(8,128)(2,1)S(1)}, u32[]{:S(2)}, u32[]{:S(2)}) %collective-permute-start.22) | collective-permute-done | bytes 159776 | tf_op jit(solution)/shard_map/ppermute | solution.py:56
  191.8 6.7 %collective-permute-start.23 = (bf16[62,8,128]{2,1,0:T(8,128)(2,1)S(1)}, bf16[62,8,128]{2,1,0:T(8,128)(2,1)S(1)}, u32[]{:S(2)}, u32[]{:S(2)}) collective-permute-start(bf16[62,8,128]{2,1,0:T(8,128)(2,1)S(1)} %pad_maximum_fusion.9), channel_id=1, source_target_pairs={{0,8},{2,10},{4,12},{6,14},{8,0},{10,2},{12,4},{14,6},{1,9},{3,11}... | collective-permute-start | bytes 380936 | tf_op jit(solution)/shard_map/ppermute | solution.py:56
  200.1 1.4 collective-permute-done.23
  201.6 4.2 %collective-permute-start.24 = (f32[46,8,128]{2,1,0:T(8,128)S(1)}, f32[46,8,128]{2,1,0:T(8,128)S(1)}, u32[]{:S(2)}, u32[]{:S(2)}) collective-permute-start(f32[46,8,128]{2,1,0:T(8,128)S(1)} %slice_add_fusion.2), channel_id=1, source_target_pairs={{0,1},{1,0},{2,3},{3,2},{4,5},{5,4},{6,7},{7,6},{8,9},{9,8},{10,11... | collective-permute-start | bytes 565256 | tf_op jit(solution)/shard_map/ppermute | solution.py:60
  (115 shorter events, 20.5 us)
Async XLA Ops:
  0.6 23.0 %copy-start.14 = (f32[32,512]{1,0:T(8,128)S(1)}, f32[32,512]{1,0:T(8,128)}, u32[]{:S(2)}) copy-start(f32[32,512]{1,0:T(8,128)} %narrow.1) | copy-start | bytes 196612
  0.6 23.0 %copy-start.4 = (bf16[1848,512]{1,0:T(8,128)(2,1)S(1)}, bf16[1848,512]{1,0:T(8,128)(2,1)}, u32[]{:S(2)}) copy-start(bf16[1848,512]{1,0:T(8,128)(2,1)} %base.1) | copy-start | bytes 5677060
  0.7 16.2 %collective-permute-start = (bf16[1,32,512]{2,1,0:T(8,128)(2,1)}, bf16[1,32,512]{2,1,0:T(8,128)(2,1)S(1)}, u32[]{:S(2)}, u32[]{:S(2)}) collective-permute-start(bf16[1,32,512]{2,1,0:T(8,128)(2,1)} %bitcast.93), channel_id=1, source_target_pairs={{0,8},{2,10},{4,12},{6,14},{8,0},{10,2},{12,4},{14,6},{1,9},{3,11}... | collective-permute-start | bytes 98312 | tf_op jit(solution)/shard_map/ppermute | solution.py:56
  10.1 18.5 %all-to-all-start = ((bf16[16,32,512]{2,1,0:T(8,128)(2,1)}), bf16[16,32,512]{2,1,0:T(8,128)(2,1)S(1)}, u32[]{:S(2)}, u32[]{:S(2)}) async-start(bf16[16,32,512]{2,1,0:T(8,128)(2,1)} %broadcast_in_dim.7), calls=%async_computation | async-start | bytes 1048576 | tf_op jit(solution)/shard_map/all_to_all | solution.py:96
  17.6 5.0 %collective-permute-start.1 = (bf16[2,32,512]{2,1,0:T(8,128)(2,1)S(1)}, bf16[2,32,512]{2,1,0:T(8,128)(2,1)S(1)}, u32[]{:S(2)}, u32[]{:S(2)}) collective-permute-start(bf16[2,32,512]{2,1,0:T(8,128)(2,1)S(1)} %pad_maximum_fusion.10), channel_id=1, source_target_pairs={{0,4},{2,6},{4,0},{6,2},{8,12},{10,14},{12,8},{14,10},{1,5},{3,7},... | collective-permute-start | bytes 196616 | tf_op jit(solution)/shard_map/ppermute | solution.py:56
  23.4 4.2 %collective-permute-start.2 = (bf16[4,32,512]{2,1,0:T(8,128)(2,1)S(1)}, bf16[4,32,512]{2,1,0:T(8,128)(2,1)}, u32[]{:S(2)}, u32[]{:S(2)}) collective-permute-start(bf16[4,32,512]{2,1,0:T(8,128)(2,1)S(1)} %pad_maximum_fusion.8), channel_id=1, source_target_pairs={{0,2},{2,0},{4,6},{6,4},{8,10},{10,8},{12,14},{14,12},{1,3},{3,1},... | collective-permute-start | bytes 393224 | tf_op jit(solution)/shard_map/ppermute | solution.py:56
  24.6 15.3 %copy-start.15 = (s32[4]{0:T(128)}, s32[4]{0:T(128)S(1)}, u32[]{:S(2)}) copy-start(s32[4]{0:T(128)S(1)} %pad_add_fusion.ids) | copy-start | bytes 52
  24.6 3.1 %copy-start.22 = (bf16[32,512]{1,0:T(8,128)(2,1)S(1)}, bf16[32,512]{1,0:T(8,128)(2,1)}, u32[]{:S(2)}) copy-start(bf16[32,512]{1,0:T(8,128)(2,1)} %param.11) | copy-start | bytes 98308
  24.6 10.6 %copy-start.8 = (f32[32,1848]{1,0:T(8,128)S(1)}, f32[32,1848]{1,0:T(8,128)}, u32[]{:S(2)}) copy-start(f32[32,1848]{1,0:T(8,128)} %refs_0_.3) | copy-start | bytes 709636
  24.6 10.6 %copy-start.9 = (f32[32,1848]{1,0:T(8,128)S(1)}, f32[32,1848]{1,0:T(8,128)}, u32[]{:S(2)}) copy-start(f32[32,1848]{1,0:T(8,128)} %refs_1_.3) | copy-start | bytes 709636
  24.6 10.6 %copy-start.12 = (f32[32,512]{1,0:T(8,128)S(1)}, f32[32,512]{1,0:T(8,128)}, u32[]{:S(2)}) copy-start(f32[32,512]{1,0:T(8,128)} %refs_2_.5) | copy-start | bytes 196612
  24.6 10.6 %copy-start.13 = (f32[32,512]{1,0:T(8,128)S(1)}, f32[32,512]{1,0:T(8,128)}, u32[]{:S(2)}) copy-start(f32[32,512]{1,0:T(8,128)} %refs_3_.3) | copy-start | bytes 196612
  27.1 8.1 %copy-start = (bf16[512,1848]{0,1:T(8,128)(2,1)S(1)}, bf16[512,1848]{0,1:T(8,128)(2,1)}, u32[]{:S(2)}) copy-start(bf16[512,1848]{0,1:T(8,128)(2,1)} %param.13) | copy-start | bytes 5677060
  30.1 8.3 %copy-start.7 = (bf16[16,32,512]{2,1,0:T(8,128)(2,1)}, bf16[16,32,512]{2,1,0:T(8,128)(2,1)S(1)}, u32[]{:S(2)}) copy-start(bf16[16,32,512]{2,1,0:T(8,128)(2,1)S(1)} %all-to-all-done.cot) | copy-start | bytes 1572868
  32.0 6.5 %collective-permute-start.4 = (bf16[8,32,1848]{2,1,0:T(8,128)(2,1)S(1)}, bf16[8,32,1848]{2,1,0:T(8,128)(2,1)S(1)}, u32[]{:S(2)}, u32[]{:S(2)}) collective-permute-start(bf16[8,32,1848]{2,1,0:T(8,128)(2,1)S(1)} %get-tuple-element.33), channel_id=1, source_target_pairs={{0,1},{1,0},{2,3},{3,2},{4,5},{5,4},{6,7},{7,6},{8,9},{9,8},{10,11... | collective-permute-start | bytes 2838536 | tf_op jit(solution)/shard_map/ppermute | solution.py:60
  35.1 4.8 %collective-permute-start.3 = (bf16[8,32,512]{2,1,0:T(8,128)(2,1)S(1)}, bf16[8,32,512]{2,1,0:T(8,128)(2,1)S(1)}, u32[]{:S(2)}, u32[]{:S(2)}) collective-permute-start(bf16[8,32,512]{2,1,0:T(8,128)(2,1)S(1)} %pad_maximum_fusion.2.act_own), channel_id=1, source_target_pairs={{0,1},{1,0},{2,3},{3,2},{4,5},{5,4},{6,7},{7,6},{8,9},{9,8},{10,11... | collective-permute-start | bytes 786440 | tf_op jit(solution)/shard_map/ppermute | solution.py:60
  38.4 5.6 %copy-start.2 = (bf16[1848,512]{1,0:T(8,128)(2,1)}, bf16[1848,512]{1,0:T(8,128)(2,1)S(1)}, u32[]{:S(2)}) copy-start(bf16[1848,512]{1,0:T(8,128)(2,1)S(1)} %get-tuple-element.29.gate_eff) | copy-start | bytes 5677060
  38.5 5.6 %copy-start.3 = (bf16[1848,512]{1,0:T(8,128)(2,1)}, bf16[1848,512]{1,0:T(8,128)(2,1)S(1)}, u32[]{:S(2)}) copy-start(bf16[1848,512]{1,0:T(8,128)(2,1)S(1)} %get-tuple-element.30.up_eff) | copy-start | bytes 5677060
  44.9 15.0 %collective-permute-start.6 = (bf16[4,2,32,1848]{3,2,1,0:T(8,128)(2,1)}, bf16[4,2,32,1848]{3,2,1,0:T(8,128)(2,1)}, u32[]{:S(2)}, u32[]{:S(2)}) collective-permute-start(bf16[4,2,32,1848]{3,2,1,0:T(8,128)(2,1)} %get-tuple-element.38), channel_id=1, source_target_pairs={{0,16},{1,65},{16,32},{17,81},{32,48},{33,97},{48,0},{49,113},{64,... | collective-permute-start | bytes 2838536 | tf_op jit(solution)/shard_map/ppermute | solution.py:44
  46.5 25.0 %collective-permute-start.7 = (bf16[4,2,32,1848]{3,2,1,0:T(8,128)(2,1)}, bf16[4,2,32,1848]{3,2,1,0:T(8,128)(2,1)}, u32[]{:S(2)}, u32[]{:S(2)}) collective-permute-start(bf16[4,2,32,1848]{3,2,1,0:T(8,128)(2,1)} %get-tuple-element.39), channel_id=1, source_target_pairs={{0,32},{1,129},{16,48},{17,145},{32,0},{33,161},{48,16},{49,177},{... | collective-permute-start | bytes 2838536 | tf_op jit(solution)/shard_map/ppermute | solution.py:44
  48.9 22.6 %collective-permute-start.8 = (bf16[4,2,32,1848]{3,2,1,0:T(8,128)(2,1)S(1)}, bf16[4,2,32,1848]{3,2,1,0:T(8,128)(2,1)}, u32[]{:S(2)}, u32[]{:S(2)}) collective-permute-start(bf16[4,2,32,1848]{3,2,1,0:T(8,128)(2,1)S(1)} %get-tuple-element.40), channel_id=1, source_target_pairs={{0,48},{1,193},{16,0},{17,209},{32,16},{33,225},{48,32},{49,241},{... | collective-permute-start | bytes 2838536 | tf_op jit(solution)/shard_map/ppermute | solution.py:44
  50.1 31.3 %all-to-all-start.1 = ((bf16[8,32,1848]{2,1,0:T(8,128)(2,1)}), bf16[8,32,1848]{2,1,0:T(8,128)(2,1)S(1)}, u32[]{:S(2)}, u32[]{:S(2)}) async-start(bf16[8,32,1848]{2,1,0:T(8,128)(2,1)} %add_convert_fusion), calls=%async_computation.1 | async-start | bytes 1966080 | tf_op jit(solution)/shard_map/all_to_all | solution.py:96
  73.6 11.6 %collective-permute-start.9 = (bf16[2,32,1848]{2,1,0:T(8,128)(2,1)S(1)}, bf16[2,32,1848]{2,1,0:T(8,128)(2,1)S(1)}, u32[]{:S(2)}, u32[]{:S(2)}) collective-permute-start(bf16[2,32,1848]{2,1,0:T(8,128)(2,1)S(1)} %get-tuple-element.51), channel_id=1, source_target_pairs={{0,64},{1,17},{16,80},{17,33},{32,96},{33,49},{48,112},{49,1},{64,... | collective-permute-start | bytes 709640 | tf_op jit(solution)/shard_map/ppermute | solution.py:44
  74.7 10.5 %collective-permute-start.11 = (bf16[2,32,1848]{2,1,0:T(8,128)(2,1)S(1)}, bf16[2,32,1848]{2,1,0:T(8,128)(2,1)S(1)}, u32[]{:S(2)}, u32[]{:S(2)}) collective-permute-start(bf16[2,32,1848]{2,1,0:T(8,128)(2,1)S(1)} %get-tuple-element.52), channel_id=1, source_target_pairs={{0,192},{1,49},{16,208},{17,1},{32,224},{33,17},{48,240},{49,33},{... | collective-permute-start | bytes 709640 | tf_op jit(solution)/shard_map/ppermute | solution.py:44
  76.3 8.9 %collective-permute-start.10 = (bf16[2,32,1848]{2,1,0:T(8,128)(2,1)S(1)}, bf16[2,32,1848]{2,1,0:T(8,128)(2,1)S(1)}, u32[]{:S(2)}, u32[]{:S(2)}) collective-permute-start(bf16[2,32,1848]{2,1,0:T(8,128)(2,1)S(1)} %get-tuple-element.53), channel_id=1, source_target_pairs={{0,128},{1,33},{16,144},{17,49},{32,160},{33,1},{48,176},{49,17},{... | collective-permute-start | bytes 709640 | tf_op jit(solution)/shard_map/ppermute | solution.py:44
  82.1 12.8 %collective-permute-start.5 = (bf16[32,1848]{1,0:T(8,128)(2,1)}, bf16[32,1848]{1,0:T(8,128)(2,1)S(1)}, u32[]{:S(2)}, u32[]{:S(2)}) collective-permute-start(bf16[32,1848]{1,0:T(8,128)(2,1)} %reduce_sum.12), channel_id=1, source_target_pairs={{0,224},{1,160},{2,128},{3,144},{4,80},{5,240},{6,48},{7,64},{8,0}... | collective-permute-start | bytes 354824 | tf_op jit(solution)/shard_map/ppermute | solution.py:80
  95.1 7.0 %collective-permute-start.13 = (bf16[2,32,1848]{2,1,0:T(8,128)(2,1)S(1)}, bf16[2,32,1848]{2,1,0:T(8,128)(2,1)S(1)}, u32[]{:S(2)}, u32[]{:S(2)}) collective-permute-start(bf16[2,32,1848]{2,1,0:T(8,128)(2,1)S(1)} %get-tuple-element.64), channel_id=1, source_target_pairs={{0,128},{1,33},{16,144},{17,49},{32,160},{33,1},{48,176},{49,17},{... | collective-permute-start | bytes 709640 | tf_op jit(solution)/shard_map/ppermute | solution.py:44
  95.3 8.4 %collective-permute-start.12 = (bf16[2,32,1848]{2,1,0:T(8,128)(2,1)S(1)}, bf16[2,32,1848]{2,1,0:T(8,128)(2,1)S(1)}, u32[]{:S(2)}, u32[]{:S(2)}) collective-permute-start(bf16[2,32,1848]{2,1,0:T(8,128)(2,1)S(1)} %get-tuple-element.64), channel_id=1, source_target_pairs={{0,192},{1,49},{16,208},{17,1},{32,224},{33,17},{48,240},{49,33},{... | collective-permute-start | bytes 709640 | tf_op jit(solution)/shard_map/ppermute | solution.py:44
  96.2 8.5 %collective-permute-start.14 = (bf16[2,32,1848]{2,1,0:T(8,128)(2,1)S(1)}, bf16[2,32,1848]{2,1,0:T(8,128)(2,1)S(1)}, u32[]{:S(2)}, u32[]{:S(2)}) collective-permute-start(bf16[2,32,1848]{2,1,0:T(8,128)(2,1)S(1)} %get-tuple-element.64), channel_id=1, source_target_pairs={{0,64},{1,17},{16,80},{17,33},{32,96},{33,49},{48,112},{49,1},{64,... | collective-permute-start | bytes 709640 | tf_op jit(solution)/shard_map/ppermute | solution.py:44
  96.8 14.6 %collective-permute-start.15 = (bf16[32,1848]{1,0:T(8,128)(2,1)S(1)}, bf16[32,1848]{1,0:T(8,128)(2,1)S(1)}, u32[]{:S(2)}, u32[]{:S(2)}) collective-permute-start(bf16[32,1848]{1,0:T(8,128)(2,1)S(1)} %get-tuple-element.60), channel_id=1, source_target_pairs={{224,0},{160,1},{128,2},{144,3},{80,4},{240,5},{48,6},{64,7},{0,8}... | collective-permute-start | bytes 354824 | tf_op jit(solution)/shard_map/ppermute | solution.py:84
  104.8 39.7 %copy-start.17 = (bf16[4,2,32,1848]{3,2,1,0:T(8,128)(2,1)}, bf16[4,2,32,1848]{3,2,1,0:T(8,128)(2,1)S(1)}, u32[]{:S(2)}) copy-start(bf16[4,2,32,1848]{3,2,1,0:T(8,128)(2,1)S(1)} %pad_maximum_fusion.g0) | copy-start | bytes 2838532
  112.4 31.6 %all-to-all-start.2 = ((bf16[8,32,1848]{2,1,0:T(8,128)(2,1)}), bf16[8,32,1848]{2,1,0:T(8,128)(2,1)S(1)}, u32[]{:S(2)}, u32[]{:S(2)}) async-start(bf16[8,32,1848]{2,1,0:T(8,128)(2,1)} %broadcast_in_dim.8), calls=%async_computation.2 | async-start | bytes 1966080 | tf_op jit(solution)/shard_map/all_to_all | solution.py:96
  116.2 28.3 %collective-permute-start.18 = (bf16[4,2,32,1848]{3,2,1,0:T(8,128)(2,1)S(1)}, bf16[4,2,32,1848]{3,2,1,0:T(8,128)(2,1)}, u32[]{:S(2)}, u32[]{:S(2)}) collective-permute-start(bf16[4,2,32,1848]{3,2,1,0:T(8,128)(2,1)S(1)} %pad_maximum_fusion.g0), channel_id=1, source_target_pairs={{0,16},{1,65},{16,32},{17,81},{32,48},{33,97},{48,0},{49,113},{64,... | collective-permute-start | bytes 2838536 | tf_op jit(solution)/shard_map/ppermute | solution.py:44
  116.2 28.3 %collective-permute-start.17 = (bf16[4,2,32,1848]{3,2,1,0:T(8,128)(2,1)S(1)}, bf16[4,2,32,1848]{3,2,1,0:T(8,128)(2,1)}, u32[]{:S(2)}, u32[]{:S(2)}) collective-permute-start(bf16[4,2,32,1848]{3,2,1,0:T(8,128)(2,1)S(1)} %pad_maximum_fusion.g0), channel_id=1, source_target_pairs={{0,32},{1,129},{16,48},{17,145},{32,0},{33,161},{48,16},{49,177},{... | collective-permute-start | bytes 2838536 | tf_op jit(solution)/shard_map/ppermute | solution.py:44
  117.4 27.1 %collective-permute-start.16 = (bf16[4,2,32,1848]{3,2,1,0:T(8,128)(2,1)S(1)}, bf16[4,2,32,1848]{3,2,1,0:T(8,128)(2,1)}, u32[]{:S(2)}, u32[]{:S(2)}) collective-permute-start(bf16[4,2,32,1848]{3,2,1,0:T(8,128)(2,1)S(1)} %pad_maximum_fusion.g0), channel_id=1, source_target_pairs={{0,48},{1,193},{16,0},{17,209},{32,16},{33,225},{48,32},{49,241},{... | collective-permute-start | bytes 2838536 | tf_op jit(solution)/shard_map/ppermute | solution.py:44
  144.0 14.1 %copy-start.16 = (bf16[8,32,1848]{2,1,0:T(8,128)(2,1)}, bf16[8,32,1848]{2,1,0:T(8,128)(2,1)S(1)}, u32[]{:S(2)}) copy-start(bf16[8,32,1848]{2,1,0:T(8,128)(2,1)S(1)} %all-to-all-done.2.hid_own) | copy-start | bytes 2838532
  144.0 15.4 %collective-permute-start.19 = (bf16[8,32,1848]{2,1,0:T(8,128)(2,1)S(1)}, bf16[8,32,1848]{2,1,0:T(8,128)(2,1)S(1)}, u32[]{:S(2)}, u32[]{:S(2)}) collective-permute-start(bf16[8,32,1848]{2,1,0:T(8,128)(2,1)S(1)} %all-to-all-done.2.hid_own), channel_id=1, source_target_pairs={{0,1},{1,0},{2,3},{3,2},{4,5},{5,4},{6,7},{7,6},{8,9},{9,8},{10,11... | collective-permute-start | bytes 2838536 | tf_op jit(solution)/shard_map/ppermute | solution.py:60
  159.4 7.0 %copy-start.20 = (f32[32,8,128]{2,1,0:T(8,128)S(1)}, f32[32,8,128]{2,1,0:T(8,128)}, u32[]{:S(2)}) copy-start(f32[32,8,128]{2,1,0:T(8,128)} %get-tuple-element.46) | copy-start | bytes 393220
  167.5 7.6 %collective-permute-start.20 = (f32[174,8,128]{2,1,0:T(8,128)S(1)}, f32[174,8,128]{2,1,0:T(8,128)S(1)}, u32[]{:S(2)}, u32[]{:S(2)}) collective-permute-start(f32[174,8,128]{2,1,0:T(8,128)S(1)} %pad_maximum_fusion.1), channel_id=1, source_target_pairs={{0,1},{1,0},{2,3},{3,2},{4,5},{5,4},{6,7},{7,6},{8,9},{9,8},{10,11... | collective-permute-start | bytes 2138120 | tf_op jit(solution)/shard_map/ppermute | solution.py:60
  168.4 6.7 %copy-start.18 = (f32[60,8,128]{2,1,0:T(8,128)S(1)}, f32[60,8,128]{2,1,0:T(8,128)}, u32[]{:S(2)}) copy-start(f32[60,8,128]{2,1,0:T(8,128)} %get-tuple-element.45) | copy-start | bytes 737284
  168.5 5.8 %collective-permute-start.25 = (bf16[136,8,128]{2,1,0:T(8,128)(2,1)S(1)}, bf16[136,8,128]{2,1,0:T(8,128)(2,1)S(1)}, u32[]{:S(2)}, u32[]{:S(2)}) collective-permute-start(bf16[136,8,128]{2,1,0:T(8,128)(2,1)S(1)} %convert_element_type.185), channel_id=1, source_target_pairs={{0,16},{1,65},{16,0},{17,81},{32,48},{33,97},{48,32},{49,113},{64,... | collective-permute-start | bytes 835592 | tf_op jit(solution)/shard_map/ppermute | solution.py:44
  174.3 7.3 %collective-permute-start.26 = (bf16[136,8,128]{2,1,0:T(8,128)(2,1)S(1)}, bf16[136,8,128]{2,1,0:T(8,128)(2,1)S(1)}, u32[]{:S(2)}, u32[]{:S(2)}) collective-permute-start(bf16[136,8,128]{2,1,0:T(8,128)(2,1)S(1)} %fusion.2), channel_id=1, source_target_pairs={{0,32},{1,129},{16,48},{17,145},{32,0},{33,161},{48,16},{49,177},{... | collective-permute-start | bytes 835592 | tf_op jit(solution)/shard_map/ppermute | solution.py:44
  175.3 7.0 %collective-permute-start.21 = (bf16[110,8,128]{2,1,0:T(8,128)(2,1)S(1)}, bf16[110,8,128]{2,1,0:T(8,128)(2,1)S(1)}, u32[]{:S(2)}, u32[]{:S(2)}) collective-permute-start(bf16[110,8,128]{2,1,0:T(8,128)(2,1)S(1)} %pad_maximum_fusion.5), channel_id=1, source_target_pairs={{0,2},{2,0},{4,6},{6,4},{8,10},{10,8},{12,14},{14,12},{1,3},{3,1},... | collective-permute-start | bytes 675848 | tf_op jit(solution)/shard_map/ppermute | solution.py:56
  181.7 5.8 %collective-permute-start.27 = (bf16[136,8,128]{2,1,0:T(8,128)(2,1)S(1)}, bf16[136,8,128]{2,1,0:T(8,128)(2,1)S(1)}, u32[]{:S(2)}, u32[]{:S(2)}) collective-permute-start(bf16[136,8,128]{2,1,0:T(8,128)(2,1)S(1)} %fusion.19), channel_id=1, source_target_pairs={{0,64},{1,17},{16,80},{17,1},{32,96},{33,49},{48,112},{49,33},{64,... | collective-permute-start | bytes 835592 | tf_op jit(solution)/shard_map/ppermute | solution.py:44
  182.4 9.3 %collective-permute-start.22 = (bf16[78,8,128]{2,1,0:T(8,128)(2,1)S(1)}, bf16[78,8,128]{2,1,0:T(8,128)(2,1)S(1)}, u32[]{:S(2)}, u32[]{:S(2)}) collective-permute-start(bf16[78,8,128]{2,1,0:T(8,128)(2,1)S(1)} %pad_maximum_fusion.7), channel_id=1, source_target_pairs={{0,4},{2,6},{4,0},{6,2},{8,12},{10,14},{12,8},{14,10},{1,5},{3,7},... | collective-permute-start | bytes 479240 | tf_op jit(solution)/shard_map/ppermute | solution.py:56
  187.6 10.9 %collective-permute-start.28 = (bf16[136,8,128]{2,1,0:T(8,128)(2,1)S(1)}, bf16[136,8,128]{2,1,0:T(8,128)(2,1)S(1)}, u32[]{:S(2)}, u32[]{:S(2)}) collective-permute-start(bf16[136,8,128]{2,1,0:T(8,128)(2,1)S(1)} %fusion.3), channel_id=1, source_target_pairs={{0,128},{1,33},{16,144},{17,49},{32,160},{33,1},{48,176},{49,17},{... | collective-permute-start | bytes 835592 | tf_op jit(solution)/shard_map/ppermute | solution.py:44
  191.8 9.7 %collective-permute-start.23 = (bf16[62,8,128]{2,1,0:T(8,128)(2,1)S(1)}, bf16[62,8,128]{2,1,0:T(8,128)(2,1)S(1)}, u32[]{:S(2)}, u32[]{:S(2)}) collective-permute-start(bf16[62,8,128]{2,1,0:T(8,128)(2,1)S(1)} %pad_maximum_fusion.9), channel_id=1, source_target_pairs={{0,8},{2,10},{4,12},{6,14},{8,0},{10,2},{12,4},{14,6},{1,9},{3,11}... | collective-permute-start | bytes 380936 | tf_op jit(solution)/shard_map/ppermute | solution.py:56
  201.6 5.3 %collective-permute-start.24 = (f32[46,8,128]{2,1,0:T(8,128)S(1)}, f32[46,8,128]{2,1,0:T(8,128)S(1)}, u32[]{:S(2)}, u32[]{:S(2)}) collective-permute-start(f32[46,8,128]{2,1,0:T(8,128)S(1)} %slice_add_fusion.2), channel_id=1, source_target_pairs={{0,1},{1,0},{2,3},{3,2},{4,5},{5,4},{6,7},{7,6},{8,9},{9,8},{10,11... | collective-permute-start | bytes 565256 | tf_op jit(solution)/shard_map/ppermute | solution.py:60
  (8 other events, 11.1 us)
